TPU v7x, 256 devices: a whole 4x4x8 slice. The times are simulated.
256 devices in a mesh: chord: 32 (over z, x), span: 8 (over y, core).
Axes of the slice: x: 4, y: 4, z: 8, core: 2. Of those that a mesh axis runs over, the one named last changes fastest.
Arguments:
- residual: float32 [5, 4, 1024, 1024], P(None, None, 'chord', 'span'), may hold values from -6 to 6
- pivot_inverse: bfloat16 [5, 5, 4, 1024, 1024], P(None, None, None, 'chord', 'span'), may hold values from -0.15 to 2, as said below
- lower_coupling: bfloat16 [5, 5, 4, 1024, 1024], P(None, None, None, 'chord', 'span'), may hold values from -1 to 0.025, as said below
- upper_coupling: bfloat16 [5, 5, 4, 1024, 1024], P(None, None, None, 'chord', 'span'), may hold values from -1 to 0.025, as said below
- span_pivot: float32 [5, 4, 1024, 1024], P(None, None, 'chord', 'span'), may hold values from 0.5 to 2
- span_lower: float32 [5, 4, 1024, 1024], P(None, None, 'chord', 'span'), may hold values from -1 to -0.8
- span_upper: float32 [5, 4, 1024, 1024], P(None, None, 'chord', 'span'), may hold values from -1 to -0.8
- normal_pivot: bfloat16 [5, 4, 1024, 1024], P(None, None, 'chord', 'span'), may hold values from 0.5 to 2
- normal_lower: bfloat16 [5, 4, 1024, 1024], P(None, None, 'chord', 'span'), may hold values from -0.8984375 to -0.19921875
- normal_upper: bfloat16 [5, 4, 1024, 1024], P(None, None, 'chord', 'span'), may hold values from -0.84765625 to -0.25
Outputs:
- update: float32 [5, 4, 1024, 1024], P(None, None, 'chord', 'span')
Inputs may be any that keep to these rules, and one draw needn't show every extreme that they name: `pivot_inverse`: diagonal entries of each block are between 0.5 and 2; off-diagonal entries have magnitude at most 0.15. `lower_coupling`: diagonal entries of each block are between -1 and -0.8; off-diagonal entries have magnitude at most 0.025. `upper_coupling`: diagonal entries of each block are between -1 and -0.8; off-diagonal entries have magnitude at most 0.025.
All inputs are finite; a program needn't handle non-finite values.
Results may differ from a plain program's by a relative error of at most 0.0003.
Values sent between devices are 32-bit elements; how exact they have to be, the bound alone decides.
A program may use at most 192 MiB of HBM per device.

v0:
```python
import jax
import jax.numpy as jnp
from jax import lax
from jax.sharding import PartitionSpec as P


def from_behind(shard, axis, by):
    count = lax.axis_size(axis)
    pairs = [(i, i + by) for i in range(count) if 0 <= i + by < count]
    return lax.ppermute(shard, axis, pairs)


def product(matrix, other):
    total = matrix[:, 0:1] * other[0:1]
    for index in range(1, matrix.shape[1]):
        total = total + matrix[:, index : index + 1] * other[index : index + 1]
    return total


def doubling_prefix(gain, shift, reverse):
    length = gain.shape[-1]
    reach = 1
    while reach < length:
        ones = jnp.ones(gain.shape[:-1] + (reach,), jnp.float32)
        zeros = jnp.zeros(shift.shape[:-1] + (reach,), jnp.float32)
        if reverse:
            early_gain = jnp.concatenate([gain[..., reach:], ones], axis=-1)
            early_shift = jnp.concatenate([shift[..., reach:], zeros], axis=-1)
        else:
            early_gain = jnp.concatenate([ones, gain[..., :-reach]], axis=-1)
            early_shift = jnp.concatenate([zeros, shift[..., :-reach]], axis=-1)
        gain, shift = (gain * early_gain, gain * early_shift + shift)
        reach = reach * 2
    return (gain, shift)


def block_end_map(coeffs, sources, order):
    first = order[0]
    matrix = coeffs[:, :, :, first]
    vector = sources[:, :, :, first]
    for cell in order[1:]:
        step = coeffs[:, :, :, cell]
        matrix = product(step, matrix)
        vector = product(step, vector) + sources[:, :, :, cell]
    return (matrix, vector)


def block_sweep(coeffs, sources, entry, order):
    values = [None] * len(order)
    state = entry
    for cell in order:
        state = product(coeffs[:, :, :, cell], state) + sources[:, :, :, cell]
        values[cell] = state
    return jnp.stack(values, axis=3)


def normal_solve(values, pivots, lowers, uppers):
    pivots = pivots.astype(jnp.float32)
    lowers = lowers.astype(jnp.float32)
    uppers = uppers.astype(jnp.float32)
    planes = []
    carry = jnp.zeros_like(values[:, 0])
    for plane in range(values.shape[1]):
        carry = pivots[:, plane] * values[:, plane] - lowers[:, plane] * carry
        planes.append(carry)
    results = [None] * values.shape[1]
    carry = jnp.zeros_like(values[:, 0])
    for plane in reversed(range(values.shape[1])):
        carry = planes[plane] - uppers[:, plane] * carry
        results[plane] = carry
    return jnp.stack(results, axis=1)


def solve_lines(pieces):
    values, pivots, lowers, uppers = pieces
    down_gain, down_shift = doubling_prefix(-lowers, pivots * values, False)
    up_gain, up_shift = doubling_prefix(-uppers, down_shift, True)
    return lax.all_to_all(up_shift, "span", split_axis=3, concat_axis=2, tiled=True)


def on_device(
    residual,
    pivot_inverse,
    lower_coupling,
    upper_coupling,
    span_pivot,
    span_lower,
    span_upper,
    normal_pivot,
    normal_lower,
    normal_upper,
):
    cells = residual.shape[2]
    ahead = list(range(cells))
    behind = list(reversed(range(cells)))
    source = product(pivot_inverse.astype(jnp.float32), residual[:, None])
    lower_terms = -lower_coupling.astype(jnp.float32)
    last_mat, last_vec = block_end_map(lower_terms, source, ahead)
    chord_count = lax.axis_size("chord")

    def relay_forward(turn, entry):
        return from_behind(product(last_mat, entry) + last_vec, "chord", 1)

    entry_down = lax.fori_loop(0, chord_count - 1, relay_forward, jnp.zeros_like(last_vec))
    forward = block_sweep(lower_terms, source, entry_down, ahead)
    upper_terms = -upper_coupling.astype(jnp.float32)
    head_mat, head_vec = block_end_map(upper_terms, forward, behind)

    def relay_backward(turn, entry):
        return from_behind(product(head_mat, entry) + head_vec, "chord", -1)

    entry_up = lax.fori_loop(0, chord_count - 1, relay_backward, jnp.zeros_like(head_vec))
    chord_part = block_sweep(upper_terms, forward, entry_up, behind)[:, 0]
    spanned = solve_lines(
        (
            lax.all_to_all(chord_part, "span", split_axis=2, concat_axis=3, tiled=True),
            lax.all_to_all(span_pivot, "span", split_axis=2, concat_axis=3, tiled=True),
            lax.all_to_all(span_lower, "span", split_axis=2, concat_axis=3, tiled=True),
            lax.all_to_all(span_upper, "span", split_axis=2, concat_axis=3, tiled=True),
        )
    )
    return normal_solve(spanned, normal_pivot, normal_lower, normal_upper)


def solution(mesh):
    return jax.shard_map(
        on_device,
        mesh=mesh,
        in_specs=(
            P(None, None, "chord", "span"),
            P(None, None, None, "chord", "span"),
            P(None, None, None, "chord", "span"),
            P(None, None, None, "chord", "span"),
            P(None, None, "chord", "span"),
            P(None, None, "chord", "span"),
            P(None, None, "chord", "span"),
            P(None, None, "chord", "span"),
            P(None, None, "chord", "span"),
            P(None, None, "chord", "span"),
        ),
        out_specs=P(None, None, "chord", "span"),
        check_vma=False,
    )
```

profile of v0, /device:TPU:102, one launch (start us, length us, event | category | flops | bytes accessed | tf_op | source)
XLA Modules:
  0.0 741.2 jit_solution(12491510379463427639)
XLA Ops:
  32.8 273.7 %while.20 = (s32[]{:T(128)}, f32[5,1,4,128]{3,2,1,0:T(4,128)S(1)}, f32[5,5,4,128]{3,2,1,0:T(4,128)S(1)}, f32[5,1,4,128]{3,2,1,0:T(4,128)S(1)}, s32[]{:T(128)}) while((s32[]{:T(128)}, f32[5,1,4,128]{3,2,1,0:T(4,128)S(1)}, f32[5,5,4,128]{3,2,1,0:T(4,128)S(1)}, f32[5,1,4,128]{3,2,1,0:T(4,128)S(1)}, s32[]{:T(128)}) %tuple.1192), condition=%wide.region_1.0_spmd, body=%wide.region_0.0_spmd.sunk | while | flops 25602 | bytes 143461 | solution.py:104
  39.2 7.5 %collective-permute-start = (f32[5,1,4,128]{3,2,1,0:T(4,128)S(1)}, f32[5,1,4,128]{3,2,1,0:T(4,128)S(1)}, u32[]{:S(2)}, u32[]{:S(2)}) collective-permute-start(f32[5,1,4,128]{3,2,1,0:T(4,128)S(1)} %add_add_fusion.125), channel_id=1, source_target_pairs={{0,8},{8,16},{16,24},{24,32},{32,40},{40,48},{48,56},{56,64},{64,7... | collective-permute-start | bytes 30728 | tf_op jit(solution)/shard_map/while/body/eval_jaxpr/ppermute | solution.py:10
  48.1 7.5 %collective-permute-start = (f32[5,1,4,128]{3,2,1,0:T(4,128)S(1)}, f32[5,1,4,128]{3,2,1,0:T(4,128)S(1)}, u32[]{:S(2)}, u32[]{:S(2)}) collective-permute-start(f32[5,1,4,128]{3,2,1,0:T(4,128)S(1)} %add_add_fusion.125), channel_id=1, source_target_pairs={{0,8},{8,16},{16,24},{24,32},{32,40},{40,48},{48,56},{56,64},{64,7... | collective-permute-start | bytes 30728 | tf_op jit(solution)/shard_map/while/body/eval_jaxpr/ppermute | solution.py:10
  57.0 7.5 %collective-permute-start = (f32[5,1,4,128]{3,2,1,0:T(4,128)S(1)}, f32[5,1,4,128]{3,2,1,0:T(4,128)S(1)}, u32[]{:S(2)}, u32[]{:S(2)}) collective-permute-start(f32[5,1,4,128]{3,2,1,0:T(4,128)S(1)} %add_add_fusion.125), channel_id=1, source_target_pairs={{0,8},{8,16},{16,24},{24,32},{32,40},{40,48},{48,56},{56,64},{64,7... | collective-permute-start | bytes 30728 | tf_op jit(solution)/shard_map/while/body/eval_jaxpr/ppermute | solution.py:10
  65.9 7.5 %collective-permute-start = (f32[5,1,4,128]{3,2,1,0:T(4,128)S(1)}, f32[5,1,4,128]{3,2,1,0:T(4,128)S(1)}, u32[]{:S(2)}, u32[]{:S(2)}) collective-permute-start(f32[5,1,4,128]{3,2,1,0:T(4,128)S(1)} %add_add_fusion.125), channel_id=1, source_target_pairs={{0,8},{8,16},{16,24},{24,32},{32,40},{40,48},{48,56},{56,64},{64,7... | collective-permute-start | bytes 30728 | tf_op jit(solution)/shard_map/while/body/eval_jaxpr/ppermute | solution.py:10
  74.8 7.5 %collective-permute-start = (f32[5,1,4,128]{3,2,1,0:T(4,128)S(1)}, f32[5,1,4,128]{3,2,1,0:T(4,128)S(1)}, u32[]{:S(2)}, u32[]{:S(2)}) collective-permute-start(f32[5,1,4,128]{3,2,1,0:T(4,128)S(1)} %add_add_fusion.125), channel_id=1, source_target_pairs={{0,8},{8,16},{16,24},{24,32},{32,40},{40,48},{48,56},{56,64},{64,7... | collective-permute-start | bytes 30728 | tf_op jit(solution)/shard_map/while/body/eval_jaxpr/ppermute | solution.py:10
  83.7 7.5 %collective-permute-start = (f32[5,1,4,128]{3,2,1,0:T(4,128)S(1)}, f32[5,1,4,128]{3,2,1,0:T(4,128)S(1)}, u32[]{:S(2)}, u32[]{:S(2)}) collective-permute-start(f32[5,1,4,128]{3,2,1,0:T(4,128)S(1)} %add_add_fusion.125), channel_id=1, source_target_pairs={{0,8},{8,16},{16,24},{24,32},{32,40},{40,48},{48,56},{56,64},{64,7... | collective-permute-start | bytes 30728 | tf_op jit(solution)/shard_map/while/body/eval_jaxpr/ppermute | solution.py:10
  92.6 7.5 %collective-permute-start = (f32[5,1,4,128]{3,2,1,0:T(4,128)S(1)}, f32[5,1,4,128]{3,2,1,0:T(4,128)S(1)}, u32[]{:S(2)}, u32[]{:S(2)}) collective-permute-start(f32[5,1,4,128]{3,2,1,0:T(4,128)S(1)} %add_add_fusion.125), channel_id=1, source_target_pairs={{0,8},{8,16},{16,24},{24,32},{32,40},{40,48},{48,56},{56,64},{64,7... | collective-permute-start | bytes 30728 | tf_op jit(solution)/shard_map/while/body/eval_jaxpr/ppermute | solution.py:10
  101.6 7.5 %collective-permute-start = (f32[5,1,4,128]{3,2,1,0:T(4,128)S(1)}, f32[5,1,4,128]{3,2,1,0:T(4,128)S(1)}, u32[]{:S(2)}, u32[]{:S(2)}) collective-permute-start(f32[5,1,4,128]{3,2,1,0:T(4,128)S(1)} %add_add_fusion.125), channel_id=1, source_target_pairs={{0,8},{8,16},{16,24},{24,32},{32,40},{40,48},{48,56},{56,64},{64,7... | collective-permute-start | bytes 30728 | tf_op jit(solution)/shard_map/while/body/eval_jaxpr/ppermute | solution.py:10
  110.5 7.5 %collective-permute-start = (f32[5,1,4,128]{3,2,1,0:T(4,128)S(1)}, f32[5,1,4,128]{3,2,1,0:T(4,128)S(1)}, u32[]{:S(2)}, u32[]{:S(2)}) collective-permute-start(f32[5,1,4,128]{3,2,1,0:T(4,128)S(1)} %add_add_fusion.125), channel_id=1, source_target_pairs={{0,8},{8,16},{16,24},{24,32},{32,40},{40,48},{48,56},{56,64},{64,7... | collective-permute-start | bytes 30728 | tf_op jit(solution)/shard_map/while/body/eval_jaxpr/ppermute | solution.py:10
  119.4 7.5 %collective-permute-start = (f32[5,1,4,128]{3,2,1,0:T(4,128)S(1)}, f32[5,1,4,128]{3,2,1,0:T(4,128)S(1)}, u32[]{:S(2)}, u32[]{:S(2)}) collective-permute-start(f32[5,1,4,128]{3,2,1,0:T(4,128)S(1)} %add_add_fusion.125), channel_id=1, source_target_pairs={{0,8},{8,16},{16,24},{24,32},{32,40},{40,48},{48,56},{56,64},{64,7... | collective-permute-start | bytes 30728 | tf_op jit(solution)/shard_map/while/body/eval_jaxpr/ppermute | solution.py:10
  128.3 7.5 %collective-permute-start = (f32[5,1,4,128]{3,2,1,0:T(4,128)S(1)}, f32[5,1,4,128]{3,2,1,0:T(4,128)S(1)}, u32[]{:S(2)}, u32[]{:S(2)}) collective-permute-start(f32[5,1,4,128]{3,2,1,0:T(4,128)S(1)} %add_add_fusion.125), channel_id=1, source_target_pairs={{0,8},{8,16},{16,24},{24,32},{32,40},{40,48},{48,56},{56,64},{64,7... | collective-permute-start | bytes 30728 | tf_op jit(solution)/shard_map/while/body/eval_jaxpr/ppermute | solution.py:10
  137.2 7.5 %collective-permute-start = (f32[5,1,4,128]{3,2,1,0:T(4,128)S(1)}, f32[5,1,4,128]{3,2,1,0:T(4,128)S(1)}, u32[]{:S(2)}, u32[]{:S(2)}) collective-permute-start(f32[5,1,4,128]{3,2,1,0:T(4,128)S(1)} %add_add_fusion.125), channel_id=1, source_target_pairs={{0,8},{8,16},{16,24},{24,32},{32,40},{40,48},{48,56},{56,64},{64,7... | collective-permute-start | bytes 30728 | tf_op jit(solution)/shard_map/while/body/eval_jaxpr/ppermute | solution.py:10
  146.1 7.5 %collective-permute-start = (f32[5,1,4,128]{3,2,1,0:T(4,128)S(1)}, f32[5,1,4,128]{3,2,1,0:T(4,128)S(1)}, u32[]{:S(2)}, u32[]{:S(2)}) collective-permute-start(f32[5,1,4,128]{3,2,1,0:T(4,128)S(1)} %add_add_fusion.125), channel_id=1, source_target_pairs={{0,8},{8,16},{16,24},{24,32},{32,40},{40,48},{48,56},{56,64},{64,7... | collective-permute-start | bytes 30728 | tf_op jit(solution)/shard_map/while/body/eval_jaxpr/ppermute | solution.py:10
  155.0 7.5 %collective-permute-start = (f32[5,1,4,128]{3,2,1,0:T(4,128)S(1)}, f32[5,1,4,128]{3,2,1,0:T(4,128)S(1)}, u32[]{:S(2)}, u32[]{:S(2)}) collective-permute-start(f32[5,1,4,128]{3,2,1,0:T(4,128)S(1)} %add_add_fusion.125), channel_id=1, source_target_pairs={{0,8},{8,16},{16,24},{24,32},{32,40},{40,48},{48,56},{56,64},{64,7... | collective-permute-start | bytes 30728 | tf_op jit(solution)/shard_map/while/body/eval_jaxpr/ppermute | solution.py:10
  163.9 7.5 %collective-permute-start = (f32[5,1,4,128]{3,2,1,0:T(4,128)S(1)}, f32[5,1,4,128]{3,2,1,0:T(4,128)S(1)}, u32[]{:S(2)}, u32[]{:S(2)}) collective-permute-start(f32[5,1,4,128]{3,2,1,0:T(4,128)S(1)} %add_add_fusion.125), channel_id=1, source_target_pairs={{0,8},{8,16},{16,24},{24,32},{32,40},{40,48},{48,56},{56,64},{64,7... | collective-permute-start | bytes 30728 | tf_op jit(solution)/shard_map/while/body/eval_jaxpr/ppermute | solution.py:10
  172.8 7.5 %collective-permute-start = (f32[5,1,4,128]{3,2,1,0:T(4,128)S(1)}, f32[5,1,4,128]{3,2,1,0:T(4,128)S(1)}, u32[]{:S(2)}, u32[]{:S(2)}) collective-permute-start(f32[5,1,4,128]{3,2,1,0:T(4,128)S(1)} %add_add_fusion.125), channel_id=1, source_target_pairs={{0,8},{8,16},{16,24},{24,32},{32,40},{40,48},{48,56},{56,64},{64,7... | collective-permute-start | bytes 30728 | tf_op jit(solution)/shard_map/while/body/eval_jaxpr/ppermute | solution.py:10
  181.7 7.5 %collective-permute-start = (f32[5,1,4,128]{3,2,1,0:T(4,128)S(1)}, f32[5,1,4,128]{3,2,1,0:T(4,128)S(1)}, u32[]{:S(2)}, u32[]{:S(2)}) collective-permute-start(f32[5,1,4,128]{3,2,1,0:T(4,128)S(1)} %add_add_fusion.125), channel_id=1, source_target_pairs={{0,8},{8,16},{16,24},{24,32},{32,40},{40,48},{48,56},{56,64},{64,7... | collective-permute-start | bytes 30728 | tf_op jit(solution)/shard_map/while/body/eval_jaxpr/ppermute | solution.py:10
  190.6 7.5 %collective-permute-start = (f32[5,1,4,128]{3,2,1,0:T(4,128)S(1)}, f32[5,1,4,128]{3,2,1,0:T(4,128)S(1)}, u32[]{:S(2)}, u32[]{:S(2)}) collective-permute-start(f32[5,1,4,128]{3,2,1,0:T(4,128)S(1)} %add_add_fusion.125), channel_id=1, source_target_pairs={{0,8},{8,16},{16,24},{24,32},{32,40},{40,48},{48,56},{56,64},{64,7... | collective-permute-start | bytes 30728 | tf_op jit(solution)/shard_map/while/body/eval_jaxpr/ppermute | solution.py:10
  208.5 7.5 %collective-permute-start = (f32[5,1,4,128]{3,2,1,0:T(4,128)S(1)}, f32[5,1,4,128]{3,2,1,0:T(4,128)S(1)}, u32[]{:S(2)}, u32[]{:S(2)}) collective-permute-start(f32[5,1,4,128]{3,2,1,0:T(4,128)S(1)} %add_add_fusion.125), channel_id=1, source_target_pairs={{0,8},{8,16},{16,24},{24,32},{32,40},{40,48},{48,56},{56,64},{64,7... | collective-permute-start | bytes 30728 | tf_op jit(solution)/shard_map/while/body/eval_jaxpr/ppermute | solution.py:10
  217.4 7.5 %collective-permute-start = (f32[5,1,4,128]{3,2,1,0:T(4,128)S(1)}, f32[5,1,4,128]{3,2,1,0:T(4,128)S(1)}, u32[]{:S(2)}, u32[]{:S(2)}) collective-permute-start(f32[5,1,4,128]{3,2,1,0:T(4,128)S(1)} %add_add_fusion.125), channel_id=1, source_target_pairs={{0,8},{8,16},{16,24},{24,32},{32,40},{40,48},{48,56},{56,64},{64,7... | collective-permute-start | bytes 30728 | tf_op jit(solution)/shard_map/while/body/eval_jaxpr/ppermute | solution.py:10
  235.2 7.5 %collective-permute-start = (f32[5,1,4,128]{3,2,1,0:T(4,128)S(1)}, f32[5,1,4,128]{3,2,1,0:T(4,128)S(1)}, u32[]{:S(2)}, u32[]{:S(2)}) collective-permute-start(f32[5,1,4,128]{3,2,1,0:T(4,128)S(1)} %add_add_fusion.125), channel_id=1, source_target_pairs={{0,8},{8,16},{16,24},{24,32},{32,40},{40,48},{48,56},{56,64},{64,7... | collective-permute-start | bytes 30728 | tf_op jit(solution)/shard_map/while/body/eval_jaxpr/ppermute | solution.py:10
  244.1 7.5 %collective-permute-start = (f32[5,1,4,128]{3,2,1,0:T(4,128)S(1)}, f32[5,1,4,128]{3,2,1,0:T(4,128)S(1)}, u32[]{:S(2)}, u32[]{:S(2)}) collective-permute-start(f32[5,1,4,128]{3,2,1,0:T(4,128)S(1)} %add_add_fusion.125), channel_id=1, source_target_pairs={{0,8},{8,16},{16,24},{24,32},{32,40},{40,48},{48,56},{56,64},{64,7... | collective-permute-start | bytes 30728 | tf_op jit(solution)/shard_map/while/body/eval_jaxpr/ppermute | solution.py:10
  261.9 7.5 %collective-permute-start = (f32[5,1,4,128]{3,2,1,0:T(4,128)S(1)}, f32[5,1,4,128]{3,2,1,0:T(4,128)S(1)}, u32[]{:S(2)}, u32[]{:S(2)}) collective-permute-start(f32[5,1,4,128]{3,2,1,0:T(4,128)S(1)} %add_add_fusion.125), channel_id=1, source_target_pairs={{0,8},{8,16},{16,24},{24,32},{32,40},{40,48},{48,56},{56,64},{64,7... | collective-permute-start | bytes 30728 | tf_op jit(solution)/shard_map/while/body/eval_jaxpr/ppermute | solution.py:10
  270.8 7.6 %collective-permute-start = (f32[5,1,4,128]{3,2,1,0:T(4,128)S(1)}, f32[5,1,4,128]{3,2,1,0:T(4,128)S(1)}, u32[]{:S(2)}, u32[]{:S(2)}) collective-permute-start(f32[5,1,4,128]{3,2,1,0:T(4,128)S(1)} %add_add_fusion.125), channel_id=1, source_target_pairs={{0,8},{8,16},{16,24},{24,32},{32,40},{40,48},{48,56},{56,64},{64,7... | collective-permute-start | bytes 30728 | tf_op jit(solution)/shard_map/while/body/eval_jaxpr/ppermute | solution.py:10
  279.8 7.5 %collective-permute-start = (f32[5,1,4,128]{3,2,1,0:T(4,128)S(1)}, f32[5,1,4,128]{3,2,1,0:T(4,128)S(1)}, u32[]{:S(2)}, u32[]{:S(2)}) collective-permute-start(f32[5,1,4,128]{3,2,1,0:T(4,128)S(1)} %add_add_fusion.125), channel_id=1, source_target_pairs={{0,8},{8,16},{16,24},{24,32},{32,40},{40,48},{48,56},{56,64},{64,7... | collective-permute-start | bytes 30728 | tf_op jit(solution)/shard_map/while/body/eval_jaxpr/ppermute | solution.py:10
  288.7 7.5 %collective-permute-start = (f32[5,1,4,128]{3,2,1,0:T(4,128)S(1)}, f32[5,1,4,128]{3,2,1,0:T(4,128)S(1)}, u32[]{:S(2)}, u32[]{:S(2)}) collective-permute-start(f32[5,1,4,128]{3,2,1,0:T(4,128)S(1)} %add_add_fusion.125), channel_id=1, source_target_pairs={{0,8},{8,16},{16,24},{24,32},{32,40},{40,48},{48,56},{56,64},{64,7... | collective-permute-start | bytes 30728 | tf_op jit(solution)/shard_map/while/body/eval_jaxpr/ppermute | solution.py:10
  333.3 276.7 %while.21 = (s32[]{:T(128)}, f32[5,1,4,128]{3,2,1,0:T(4,128)S(1)}, f32[5,5,4,128]{3,2,1,0:T(4,128)S(1)}, f32[5,1,4,128]{3,2,1,0:T(4,128)S(1)}, s32[]{:T(128)}) while((s32[]{:T(128)}, f32[5,1,4,128]{3,2,1,0:T(4,128)S(1)}, f32[5,5,4,128]{3,2,1,0:T(4,128)S(1)}, f32[5,1,4,128]{3,2,1,0:T(4,128)S(1)}, s32[]{:T(128)}) %tuple.1195), condition=%wide.region_3.0_spmd, body=%wide.region_2.0_spmd.sunk | while | flops 25602 | bytes 143461 | solution.py:112
  659.5 8.9 %all-to-all-done.1 = f32[5,4,32,128]{3,0,1,2:T(8,128)S(1)} async-done(((f32[5,4,32,128]{3,0,1,2:T(8,128)}), f32[5,4,32,128]{3,0,1,2:T(8,128)S(1)}, u32[]{:S(2)}, u32[]{:S(2)}) %all-to-all-start.1) | async-done | bytes 327712 | tf_op jit(solution)/shard_map/all_to_all | solution.py:118
  694.4 11.1 %reshape.1336 = f32[8,1,10240]{2,1,0:T(1,128)} reshape(f32[1024,4,4,5]{3,2,1,0:T(4,128)} %bitcast.2969) | data formatting | bytes 655360
  709.4 7.8 %all-to-all-done.4 = f32[8,1,10240]{2,1,0:T(1,128)S(1)} async-done(((f32[8,1,10240]{2,1,0:T(1,128)}), f32[8,1,10240]{2,1,0:T(1,128)S(1)}, u32[]{:S(2)}, u32[]{:S(2)}) %all-to-all-start.4) | async-done | bytes 327712 | tf_op jit(solution)/shard_map/all_to_all | solution.py:78
  719.1 14.3 %reshape.1337 = f32[1024,4,4,5]{3,2,1,0:T(4,128)} reshape(f32[8,10240]{1,0:T(8,128)S(1)} %reduce) | data formatting | bytes 655360
  (760 shorter events, 499.6 us)
Async XLA Ops:
  39.2 8.9 %collective-permute-start = (f32[5,1,4,128]{3,2,1,0:T(4,128)S(1)}, f32[5,1,4,128]{3,2,1,0:T(4,128)S(1)}, u32[]{:S(2)}, u32[]{:S(2)}) collective-permute-start(f32[5,1,4,128]{3,2,1,0:T(4,128)S(1)} %add_add_fusion.125), channel_id=1, source_target_pairs={{0,8},{8,16},{16,24},{24,32},{32,40},{40,48},{48,56},{56,64},{64,7... | collective-permute-start | bytes 30728 | tf_op jit(solution)/shard_map/while/body/eval_jaxpr/ppermute | solution.py:10
  48.1 8.9 %collective-permute-start = (f32[5,1,4,128]{3,2,1,0:T(4,128)S(1)}, f32[5,1,4,128]{3,2,1,0:T(4,128)S(1)}, u32[]{:S(2)}, u32[]{:S(2)}) collective-permute-start(f32[5,1,4,128]{3,2,1,0:T(4,128)S(1)} %add_add_fusion.125), channel_id=1, source_target_pairs={{0,8},{8,16},{16,24},{24,32},{32,40},{40,48},{48,56},{56,64},{64,7... | collective-permute-start | bytes 30728 | tf_op jit(solution)/shard_map/while/body/eval_jaxpr/ppermute | solution.py:10
  57.0 8.9 %collective-permute-start = (f32[5,1,4,128]{3,2,1,0:T(4,128)S(1)}, f32[5,1,4,128]{3,2,1,0:T(4,128)S(1)}, u32[]{:S(2)}, u32[]{:S(2)}) collective-permute-start(f32[5,1,4,128]{3,2,1,0:T(4,128)S(1)} %add_add_fusion.125), channel_id=1, source_target_pairs={{0,8},{8,16},{16,24},{24,32},{32,40},{40,48},{48,56},{56,64},{64,7... | collective-permute-start | bytes 30728 | tf_op jit(solution)/shard_map/while/body/eval_jaxpr/ppermute | solution.py:10
  65.9 8.9 %collective-permute-start = (f32[5,1,4,128]{3,2,1,0:T(4,128)S(1)}, f32[5,1,4,128]{3,2,1,0:T(4,128)S(1)}, u32[]{:S(2)}, u32[]{:S(2)}) collective-permute-start(f32[5,1,4,128]{3,2,1,0:T(4,128)S(1)} %add_add_fusion.125), channel_id=1, source_target_pairs={{0,8},{8,16},{16,24},{24,32},{32,40},{40,48},{48,56},{56,64},{64,7... | collective-permute-start | bytes 30728 | tf_op jit(solution)/shard_map/while/body/eval_jaxpr/ppermute | solution.py:10
  74.8 8.9 %collective-permute-start = (f32[5,1,4,128]{3,2,1,0:T(4,128)S(1)}, f32[5,1,4,128]{3,2,1,0:T(4,128)S(1)}, u32[]{:S(2)}, u32[]{:S(2)}) collective-permute-start(f32[5,1,4,128]{3,2,1,0:T(4,128)S(1)} %add_add_fusion.125), channel_id=1, source_target_pairs={{0,8},{8,16},{16,24},{24,32},{32,40},{40,48},{48,56},{56,64},{64,7... | collective-permute-start | bytes 30728 | tf_op jit(solution)/shard_map/while/body/eval_jaxpr/ppermute | solution.py:10
  83.7 8.9 %collective-permute-start = (f32[5,1,4,128]{3,2,1,0:T(4,128)S(1)}, f32[5,1,4,128]{3,2,1,0:T(4,128)S(1)}, u32[]{:S(2)}, u32[]{:S(2)}) collective-permute-start(f32[5,1,4,128]{3,2,1,0:T(4,128)S(1)} %add_add_fusion.125), channel_id=1, source_target_pairs={{0,8},{8,16},{16,24},{24,32},{32,40},{40,48},{48,56},{56,64},{64,7... | collective-permute-start | bytes 30728 | tf_op jit(solution)/shard_map/while/body/eval_jaxpr/ppermute | solution.py:10
  92.6 8.9 %collective-permute-start = (f32[5,1,4,128]{3,2,1,0:T(4,128)S(1)}, f32[5,1,4,128]{3,2,1,0:T(4,128)S(1)}, u32[]{:S(2)}, u32[]{:S(2)}) collective-permute-start(f32[5,1,4,128]{3,2,1,0:T(4,128)S(1)} %add_add_fusion.125), channel_id=1, source_target_pairs={{0,8},{8,16},{16,24},{24,32},{32,40},{40,48},{48,56},{56,64},{64,7... | collective-permute-start | bytes 30728 | tf_op jit(solution)/shard_map/while/body/eval_jaxpr/ppermute | solution.py:10
  101.6 8.9 %collective-permute-start = (f32[5,1,4,128]{3,2,1,0:T(4,128)S(1)}, f32[5,1,4,128]{3,2,1,0:T(4,128)S(1)}, u32[]{:S(2)}, u32[]{:S(2)}) collective-permute-start(f32[5,1,4,128]{3,2,1,0:T(4,128)S(1)} %add_add_fusion.125), channel_id=1, source_target_pairs={{0,8},{8,16},{16,24},{24,32},{32,40},{40,48},{48,56},{56,64},{64,7... | collective-permute-start | bytes 30728 | tf_op jit(solution)/shard_map/while/body/eval_jaxpr/ppermute | solution.py:10
  110.5 8.9 %collective-permute-start = (f32[5,1,4,128]{3,2,1,0:T(4,128)S(1)}, f32[5,1,4,128]{3,2,1,0:T(4,128)S(1)}, u32[]{:S(2)}, u32[]{:S(2)}) collective-permute-start(f32[5,1,4,128]{3,2,1,0:T(4,128)S(1)} %add_add_fusion.125), channel_id=1, source_target_pairs={{0,8},{8,16},{16,24},{24,32},{32,40},{40,48},{48,56},{56,64},{64,7... | collective-permute-start | bytes 30728 | tf_op jit(solution)/shard_map/while/body/eval_jaxpr/ppermute | solution.py:10
  119.4 8.9 %collective-permute-start = (f32[5,1,4,128]{3,2,1,0:T(4,128)S(1)}, f32[5,1,4,128]{3,2,1,0:T(4,128)S(1)}, u32[]{:S(2)}, u32[]{:S(2)}) collective-permute-start(f32[5,1,4,128]{3,2,1,0:T(4,128)S(1)} %add_add_fusion.125), channel_id=1, source_target_pairs={{0,8},{8,16},{16,24},{24,32},{32,40},{40,48},{48,56},{56,64},{64,7... | collective-permute-start | bytes 30728 | tf_op jit(solution)/shard_map/while/body/eval_jaxpr/ppermute | solution.py:10
  128.3 8.9 %collective-permute-start = (f32[5,1,4,128]{3,2,1,0:T(4,128)S(1)}, f32[5,1,4,128]{3,2,1,0:T(4,128)S(1)}, u32[]{:S(2)}, u32[]{:S(2)}) collective-permute-start(f32[5,1,4,128]{3,2,1,0:T(4,128)S(1)} %add_add_fusion.125), channel_id=1, source_target_pairs={{0,8},{8,16},{16,24},{24,32},{32,40},{40,48},{48,56},{56,64},{64,7... | collective-permute-start | bytes 30728 | tf_op jit(solution)/shard_map/while/body/eval_jaxpr/ppermute | solution.py:10
  137.2 8.9 %collective-permute-start = (f32[5,1,4,128]{3,2,1,0:T(4,128)S(1)}, f32[5,1,4,128]{3,2,1,0:T(4,128)S(1)}, u32[]{:S(2)}, u32[]{:S(2)}) collective-permute-start(f32[5,1,4,128]{3,2,1,0:T(4,128)S(1)} %add_add_fusion.125), channel_id=1, source_target_pairs={{0,8},{8,16},{16,24},{24,32},{32,40},{40,48},{48,56},{56,64},{64,7... | collective-permute-start | bytes 30728 | tf_op jit(solution)/shard_map/while/body/eval_jaxpr/ppermute | solution.py:10
  146.1 8.9 %collective-permute-start = (f32[5,1,4,128]{3,2,1,0:T(4,128)S(1)}, f32[5,1,4,128]{3,2,1,0:T(4,128)S(1)}, u32[]{:S(2)}, u32[]{:S(2)}) collective-permute-start(f32[5,1,4,128]{3,2,1,0:T(4,128)S(1)} %add_add_fusion.125), channel_id=1, source_target_pairs={{0,8},{8,16},{16,24},{24,32},{32,40},{40,48},{48,56},{56,64},{64,7... | collective-permute-start | bytes 30728 | tf_op jit(solution)/shard_map/while/body/eval_jaxpr/ppermute | solution.py:10
  155.0 8.9 %collective-permute-start = (f32[5,1,4,128]{3,2,1,0:T(4,128)S(1)}, f32[5,1,4,128]{3,2,1,0:T(4,128)S(1)}, u32[]{:S(2)}, u32[]{:S(2)}) collective-permute-start(f32[5,1,4,128]{3,2,1,0:T(4,128)S(1)} %add_add_fusion.125), channel_id=1, source_target_pairs={{0,8},{8,16},{16,24},{24,32},{32,40},{40,48},{48,56},{56,64},{64,7... | collective-permute-start | bytes 30728 | tf_op jit(solution)/shard_map/while/body/eval_jaxpr/ppermute | solution.py:10
  163.9 8.9 %collective-permute-start = (f32[5,1,4,128]{3,2,1,0:T(4,128)S(1)}, f32[5,1,4,128]{3,2,1,0:T(4,128)S(1)}, u32[]{:S(2)}, u32[]{:S(2)}) collective-permute-start(f32[5,1,4,128]{3,2,1,0:T(4,128)S(1)} %add_add_fusion.125), channel_id=1, source_target_pairs={{0,8},{8,16},{16,24},{24,32},{32,40},{40,48},{48,56},{56,64},{64,7... | collective-permute-start | bytes 30728 | tf_op jit(solution)/shard_map/while/body/eval_jaxpr/ppermute | solution.py:10
  172.8 8.9 %collective-permute-start = (f32[5,1,4,128]{3,2,1,0:T(4,128)S(1)}, f32[5,1,4,128]{3,2,1,0:T(4,128)S(1)}, u32[]{:S(2)}, u32[]{:S(2)}) collective-permute-start(f32[5,1,4,128]{3,2,1,0:T(4,128)S(1)} %add_add_fusion.125), channel_id=1, source_target_pairs={{0,8},{8,16},{16,24},{24,32},{32,40},{40,48},{48,56},{56,64},{64,7... | collective-permute-start | bytes 30728 | tf_op jit(solution)/shard_map/while/body/eval_jaxpr/ppermute | solution.py:10
  181.7 8.9 %collective-permute-start = (f32[5,1,4,128]{3,2,1,0:T(4,128)S(1)}, f32[5,1,4,128]{3,2,1,0:T(4,128)S(1)}, u32[]{:S(2)}, u32[]{:S(2)}) collective-permute-start(f32[5,1,4,128]{3,2,1,0:T(4,128)S(1)} %add_add_fusion.125), channel_id=1, source_target_pairs={{0,8},{8,16},{16,24},{24,32},{32,40},{40,48},{48,56},{56,64},{64,7... | collective-permute-start | bytes 30728 | tf_op jit(solution)/shard_map/while/body/eval_jaxpr/ppermute | solution.py:10
  208.5 8.9 %collective-permute-start = (f32[5,1,4,128]{3,2,1,0:T(4,128)S(1)}, f32[5,1,4,128]{3,2,1,0:T(4,128)S(1)}, u32[]{:S(2)}, u32[]{:S(2)}) collective-permute-start(f32[5,1,4,128]{3,2,1,0:T(4,128)S(1)} %add_add_fusion.125), channel_id=1, source_target_pairs={{0,8},{8,16},{16,24},{24,32},{32,40},{40,48},{48,56},{56,64},{64,7... | collective-permute-start | bytes 30728 | tf_op jit(solution)/shard_map/while/body/eval_jaxpr/ppermute | solution.py:10
  235.2 8.9 %collective-permute-start = (f32[5,1,4,128]{3,2,1,0:T(4,128)S(1)}, f32[5,1,4,128]{3,2,1,0:T(4,128)S(1)}, u32[]{:S(2)}, u32[]{:S(2)}) collective-permute-start(f32[5,1,4,128]{3,2,1,0:T(4,128)S(1)} %add_add_fusion.125), channel_id=1, source_target_pairs={{0,8},{8,16},{16,24},{24,32},{32,40},{40,48},{48,56},{56,64},{64,7... | collective-permute-start | bytes 30728 | tf_op jit(solution)/shard_map/while/body/eval_jaxpr/ppermute | solution.py:10
  244.1 8.9 %collective-permute-start = (f32[5,1,4,128]{3,2,1,0:T(4,128)S(1)}, f32[5,1,4,128]{3,2,1,0:T(4,128)S(1)}, u32[]{:S(2)}, u32[]{:S(2)}) collective-permute-start(f32[5,1,4,128]{3,2,1,0:T(4,128)S(1)} %add_add_fusion.125), channel_id=1, source_target_pairs={{0,8},{8,16},{16,24},{24,32},{32,40},{40,48},{48,56},{56,64},{64,7... | collective-permute-start | bytes 30728 | tf_op jit(solution)/shard_map/while/body/eval_jaxpr/ppermute | solution.py:10
  261.9 8.9 %collective-permute-start = (f32[5,1,4,128]{3,2,1,0:T(4,128)S(1)}, f32[5,1,4,128]{3,2,1,0:T(4,128)S(1)}, u32[]{:S(2)}, u32[]{:S(2)}) collective-permute-start(f32[5,1,4,128]{3,2,1,0:T(4,128)S(1)} %add_add_fusion.125), channel_id=1, source_target_pairs={{0,8},{8,16},{16,24},{24,32},{32,40},{40,48},{48,56},{56,64},{64,7... | collective-permute-start | bytes 30728 | tf_op jit(solution)/shard_map/while/body/eval_jaxpr/ppermute | solution.py:10
  270.8 9.0 %collective-permute-start = (f32[5,1,4,128]{3,2,1,0:T(4,128)S(1)}, f32[5,1,4,128]{3,2,1,0:T(4,128)S(1)}, u32[]{:S(2)}, u32[]{:S(2)}) collective-permute-start(f32[5,1,4,128]{3,2,1,0:T(4,128)S(1)} %add_add_fusion.125), channel_id=1, source_target_pairs={{0,8},{8,16},{16,24},{24,32},{32,40},{40,48},{48,56},{56,64},{64,7... | collective-permute-start | bytes 30728 | tf_op jit(solution)/shard_map/while/body/eval_jaxpr/ppermute | solution.py:10
  279.8 8.9 %collective-permute-start = (f32[5,1,4,128]{3,2,1,0:T(4,128)S(1)}, f32[5,1,4,128]{3,2,1,0:T(4,128)S(1)}, u32[]{:S(2)}, u32[]{:S(2)}) collective-permute-start(f32[5,1,4,128]{3,2,1,0:T(4,128)S(1)} %add_add_fusion.125), channel_id=1, source_target_pairs={{0,8},{8,16},{16,24},{24,32},{32,40},{40,48},{48,56},{56,64},{64,7... | collective-permute-start | bytes 30728 | tf_op jit(solution)/shard_map/while/body/eval_jaxpr/ppermute | solution.py:10
  288.7 8.9 %collective-permute-start = (f32[5,1,4,128]{3,2,1,0:T(4,128)S(1)}, f32[5,1,4,128]{3,2,1,0:T(4,128)S(1)}, u32[]{:S(2)}, u32[]{:S(2)}) collective-permute-start(f32[5,1,4,128]{3,2,1,0:T(4,128)S(1)} %add_add_fusion.125), channel_id=1, source_target_pairs={{0,8},{8,16},{16,24},{24,32},{32,40},{40,48},{48,56},{56,64},{64,7... | collective-permute-start | bytes 30728 | tf_op jit(solution)/shard_map/while/body/eval_jaxpr/ppermute | solution.py:10
  333.4 9.2 %collective-permute-start.1 = (f32[5,1,4,128]{3,2,1,0:T(4,128)S(1)}, f32[5,1,4,128]{3,2,1,0:T(4,128)S(1)}, u32[]{:S(2)}, u32[]{:S(2)}) collective-permute-start(f32[5,1,4,128]{3,2,1,0:T(4,128)S(1)} %add_add_fusion.126), channel_id=1, source_target_pairs={{8,0},{16,8},{24,16},{32,24},{40,32},{48,40},{56,48},{64,56},{72,6... | collective-permute-start | bytes 30728 | tf_op jit(solution)/shard_map/while/body/eval_jaxpr/ppermute | solution.py:10
  413.9 9.0 %collective-permute-start.1 = (f32[5,1,4,128]{3,2,1,0:T(4,128)S(1)}, f32[5,1,4,128]{3,2,1,0:T(4,128)S(1)}, u32[]{:S(2)}, u32[]{:S(2)}) collective-permute-start(f32[5,1,4,128]{3,2,1,0:T(4,128)S(1)} %add_add_fusion.126), channel_id=1, source_target_pairs={{8,0},{16,8},{24,16},{32,24},{40,32},{48,40},{56,48},{64,56},{72,6... | collective-permute-start | bytes 30728 | tf_op jit(solution)/shard_map/while/body/eval_jaxpr/ppermute | solution.py:10
  476.3 9.0 %collective-permute-start.1 = (f32[5,1,4,128]{3,2,1,0:T(4,128)S(1)}, f32[5,1,4,128]{3,2,1,0:T(4,128)S(1)}, u32[]{:S(2)}, u32[]{:S(2)}) collective-permute-start(f32[5,1,4,128]{3,2,1,0:T(4,128)S(1)} %add_add_fusion.126), channel_id=1, source_target_pairs={{8,0},{16,8},{24,16},{32,24},{40,32},{48,40},{56,48},{64,56},{72,6... | collective-permute-start | bytes 30728 | tf_op jit(solution)/shard_map/while/body/eval_jaxpr/ppermute | solution.py:10
  630.3 12.7 %all-to-all-start.3 = ((f32[5,4,32,128]{3,1,0,2:T(4,128)}), f32[5,4,32,128]{3,1,0,2:T(4,128)S(1)}, u32[]{:S(2)}, u32[]{:S(2)}) async-start(f32[5,4,32,128]{3,1,0,2:T(4,128)} %bitcast.1402), calls=%async_computation.3 | async-start | bytes 655360 | tf_op jit(solution)/shard_map/all_to_all | solution.py:116
  643.0 11.6 %all-to-all-start.2 = ((f32[5,4,32,128]{3,1,0,2:T(4,128)}), f32[5,4,32,128]{3,1,0,2:T(4,128)S(1)}, u32[]{:S(2)}, u32[]{:S(2)}) async-start(f32[5,4,32,128]{3,1,0,2:T(4,128)} %copy.68), calls=%async_computation.2 | async-start | bytes 655360 | tf_op jit(solution)/shard_map/all_to_all | solution.py:117
  654.6 13.8 %all-to-all-start.1 = ((f32[5,4,32,128]{3,0,1,2:T(8,128)}), f32[5,4,32,128]{3,0,1,2:T(8,128)S(1)}, u32[]{:S(2)}, u32[]{:S(2)}) async-start(f32[5,4,32,128]{3,0,1,2:T(8,128)} %copy.66), calls=%async_computation.1 | async-start | bytes 1048576 | tf_op jit(solution)/shard_map/all_to_all | solution.py:118
  668.4 13.8 %all-to-all-start = ((f32[5,4,32,128]{3,0,1,2:T(8,128)}), f32[5,4,32,128]{3,0,1,2:T(8,128)S(1)}, u32[]{:S(2)}, u32[]{:S(2)}) async-start(f32[5,4,32,128]{3,0,1,2:T(8,128)} %copy.64), calls=%async_computation | async-start | bytes 1048576 | tf_op jit(solution)/shard_map/all_to_all | solution.py:119
  705.4 11.7 %all-to-all-start.4 = ((f32[8,1,10240]{2,1,0:T(1,128)}), f32[8,1,10240]{2,1,0:T(1,128)S(1)}, u32[]{:S(2)}, u32[]{:S(2)}) async-start(f32[8,1,10240]{2,1,0:T(1,128)} %reshape.1336), calls=%async_computation.4 | async-start | bytes 655360 | tf_op jit(solution)/shard_map/all_to_all | solution.py:78
  (55 other events, 1599.9 us)
where the time goes:
time: 749 us; the launch traced here: 741 us
  starting transfers between devices  309 us (41%)
  waiting for transfers between devices  295 us (39%)
  local copies, waits for them, and re-layouts  70.4 us (9%)
  other arithmetic  62.6 us (8%)
    ppermute x62, starting transfers between devices, from_behind(): return lax.ppermute(shard, axis, pairs)  290 us
    ppermute x62, waiting for transfers between devices, from_behind(): return lax.ppermute(shard, axis, pairs)  258 us
    unnamed x75, local copies, waits for them, and re-layouts  47.6 us
    add x63, other arithmetic, block_sweep(): state = product(coeffs[:, :, :, cell], state) + sources[:, :, :, cell]  23.6 us
    add x61, other arithmetic, block_end_map(): vector = product(step, vector) + sources[:, :, :, cell]  22.4 us
  transfers between devices with their start and end apart: 67, of which 67 were waited for; matrix products, arithmetic and copies ran while one was open for 1% of the time, Pallas kernels for 0%

commit v1 on v0

v1 whole, which is shorter than its diff:
```python
import functools

import jax
import jax.numpy as jnp
from jax import lax
from jax.experimental import pallas as pl
from jax.experimental.pallas import tpu as pltpu
from jax.sharding import PartitionSpec as P

F32 = jnp.float32
MESH = pl.DeviceIdType.MESH

NV = 5
NK = 4
CHORD = 32
SPAN = 8
CELLS = 32
LANES = 128
HALF = 16
GROUPS = 11
MAT, VEC, OUT, INN, SRC = 0, 25, 30, 55, 80


def dot(lhs, rhs):
    terms = [a * b for a, b in zip(lhs, rhs)]
    while len(terms) > 1:
        terms = [terms[i] + terms[i + 1] if i + 1 < len(terms) else terms[i] for i in range(0, len(terms), 2)]
    return terms[0]


def column(matrix, index):
    return [row[index] for row in matrix]


def matmul(lhs, rhs):
    cols = [column(rhs, j) for j in range(len(rhs[0]))]
    return [[dot(row, col) for col in cols] for row in lhs]


def matvec(lhs, vec):
    return [dot(row, vec) for row in lhs]


def block_transpose(tile, sub, blk):
    for d in (4, 2, 1):
        s_bit = (sub & d) != 0
        b_bit = (blk & d) != 0
        if d == 4:
            other = pltpu.roll(pltpu.roll(tile, 4, 0), 64, 1)
        else:
            up = pltpu.roll(pltpu.roll(tile, 8 - d, 0), 16 * d, 1)
            down = pltpu.roll(pltpu.roll(tile, d, 0), 128 - 16 * d, 1)
            other = jnp.where(s_bit, down, up)
        tile = jnp.where(s_bit == b_bit, tile, other)
    return tile


def kernel(
    res_h, piv_h, low_h, upp_h, sp_h, sl_h, su_h, np_h, nl_h, nu_h,
    out_ref,
    res, piv, low, upp, spn, sln, sun, npn, nln, nun,
    pivf, lowf, uppf, source, state, comb, send1, recv1, expand, entry, total,
    send2, recv2, unsh, carry, ysweep, wnat,
    wt, pt, lt, ut, gain, pre, alp, bet, cc, aa,
    gsend, grecv, hsend, hrecv, sentry,
    load_sem, sems,
):
    me_c = lax.axis_index("chord")
    me_s = lax.axis_index("span")

    loads = []
    for n, (src, dst) in enumerate(
        [(res_h, res), (piv_h, piv), (low_h, low), (upp_h, upp), (sp_h, spn), (sl_h, sln), (su_h, sun),
         (np_h, npn), (nl_h, nln), (nu_h, nun)]
    ):
        copy = pltpu.make_async_copy(src, dst, load_sem.at[n])
        copy.start()
        loads.append(copy)

    barrier = pltpu.get_barrier_semaphore()

    def greet_chord(o, _):
        pl.semaphore_signal(barrier, inc=1, device_id={"chord": lax.rem(me_c + o, CHORD)}, device_id_type=MESH)
        return 0

    def greet_span(o, _):
        pl.semaphore_signal(barrier, inc=1, device_id={"span": lax.rem(me_s + o, SPAN)}, device_id_type=MESH)
        return 0

    lax.fori_loop(1, CHORD, greet_chord, 0)
    lax.fori_loop(1, SPAN, greet_span, 0)

    sub = lax.broadcasted_iota(jnp.int32, (8, LANES), 0)
    lane = lax.broadcasted_iota(jnp.int32, (8, LANES), 1)
    blk = lane // 16

    def widen(src, dst):
        def body(n, _):
            rows = pl.ds(pl.multiple_of(n * 128, 128), 128)
            dst[rows] = src[rows].astype(F32)
            return 0

        lax.fori_loop(0, NV * NV, body, 0)

    loads[1].wait()
    widen(piv, pivf)
    loads[2].wait()
    widen(low, lowf)
    loads[3].wait()
    widen(upp, uppf)
    loads[0].wait()

    zero = jnp.zeros((8, LANES), F32)
    one = jnp.ones((8, LANES), F32)

    def tile_of(value):
        return pl.ds(8 * value, 8)

    for r in range(NV):
        for c in range(NV):
            state[tile_of(MAT + 5 * r + c)] = one if r == c else zero
            state[tile_of(OUT + 5 * r + c)] = one if r == c else zero
            state[tile_of(INN + 5 * r + c)] = zero
        state[tile_of(VEC + r)] = zero
        state[tile_of(SRC + r)] = zero

    def block(ref, index, step):
        return ref[pl.ds(index * 128 + step, 8, stride=HALF)]

    def blocks(ref, step):
        return [[block(ref, 5 * r + c, step) for c in range(NV)] for r in range(NV)]

    def map_step(pair, _):
        for odd in range(2):
            step = 2 * pair + odd
            cells = [block(res, c, step) for c in range(NV)]
            src = [dot([block(pivf, 5 * r + c, step) for c in range(NV)], cells) for r in range(NV)]
            for r in range(NV):
                source[pl.ds(pl.multiple_of((step * NV + r) * 8, 8), 8)] = src[r]
            lows = blocks(lowf, step)
            cols = []
            for c in range(NV):
                new = matvec(lows, [state[tile_of(MAT + 5 * r + c)] for r in range(NV)])
                for r in range(NV):
                    state[tile_of(MAT + 5 * r + c)] = new[r]
                cols.append(new)
            new = matvec(lows, [state[tile_of(VEC + r)] for r in range(NV)])
            new = [n + s if odd else n - s for n, s in zip(new, src)]
            for r in range(NV):
                state[tile_of(VEC + r)] = new[r]
            cols.append(new)
            upps = blocks(uppf, step)
            for r in range(NV):
                row = [state[tile_of(OUT + 5 * r + c)] for c in range(NV)]
                for c in range(NV):
                    at = tile_of(INN + 5 * r + c)
                    state[at] = state[at] + dot(row, cols[c])
                at = tile_of(SRC + r)
                state[at] = state[at] + dot(row, cols[NV])
                for c in range(NV):
                    state[tile_of(OUT + 5 * r + c)] = dot(row, column(upps, c))
        return 0

    lax.fori_loop(0, HALF // 2, map_step, 0)

    def half(value, which):
        return state[pl.ds(8 * value + which, NK, stride=2)]

    def half_matrix(base, which):
        return [[half(base + 5 * r + c, which) for c in range(NV)] for r in range(NV)]

    def half_vector(base, which):
        return [half(base + r, which) for r in range(NV)]

    def put(value, data):
        comb[pl.ds(NK * value, NK)] = data

    mat0 = half_matrix(MAT, 0)
    vec0 = half_vector(VEC, 0)
    mat1 = half_matrix(MAT, 1)
    mats = matmul(mat1, mat0)
    vecs = matvec(mat1, vec0)
    for r in range(NV):
        for c in range(NV):
            put(MAT + 5 * r + c, mats[r][c])
        put(VEC + r, vecs[r] + half(VEC + r, 1))
    inn1 = half_matrix(INN, 1)
    part = matmul(inn1, mat0)
    tail = [t + half(SRC + r, 1) for r, t in enumerate(matvec(inn1, vec0))]
    out0 = half_matrix(OUT, 0)
    outs = matmul(out0, half_matrix(OUT, 1))
    inns = matmul(out0, part)
    srcs = matvec(out0, tail)
    for r in range(NV):
        for c in range(NV):
            put(OUT + 5 * r + c, outs[r][c])
            put(INN + 5 * r + c, inns[r][c] + half(INN + 5 * r + c, 0))
        put(SRC + r, srcs[r] + half(SRC + r, 0))
    for value in range(85, 88):
        put(value, jnp.zeros((NK, LANES), F32))

    def shuffle(k, _):
        for g in range(GROUPS):
            tile = comb[pl.ds(NK * 8 * g + k, 8, stride=NK)]
            send1[pl.ds(8 * GROUPS * k + g, 8, stride=GROUPS), 0] = block_transpose(tile, sub, blk)
        return 0

    lax.fori_loop(0, NK, shuffle, 0)

    pl.semaphore_wait(barrier, CHORD - 1 + SPAN - 1)

    def exchange(send, recv, rows, count, me, axis, at):
        def start(o, _):
            to = lax.rem(me + o, count)
            pltpu.make_async_remote_copy(
                src_ref=send.at[pl.ds(to * rows, rows)],
                dst_ref=recv.at[pl.ds(me * rows, rows)],
                send_sem=sems.at[2 * at],
                recv_sem=sems.at[2 * at + 1],
                device_id={axis: to},
                device_id_type=MESH,
            ).start()
            return 0

        lax.fori_loop(1, count, start, 0)
        recv[pl.ds(me * rows, rows)] = send[pl.ds(me * rows, rows)]

    def spread(send, recv, rows, at):
        def start(o, _):
            pltpu.make_async_remote_copy(
                src_ref=send,
                dst_ref=recv.at[pl.ds(me_s * rows, rows)],
                send_sem=sems.at[2 * at],
                recv_sem=sems.at[2 * at + 1],
                device_id={"span": lax.rem(me_s + o, SPAN)},
                device_id_type=MESH,
            ).start()
            return 0

        lax.fori_loop(1, SPAN, start, 0)
        recv[pl.ds(me_s * rows, rows)] = send[...]

    def settle(ref, rows, sem):
        whole = ref.at[pl.ds(0, rows)]
        pltpu.make_async_copy(whole, whole, sems.at[sem]).wait()

    exchange(send1, recv1, GROUPS, CHORD, me_c, "chord", 0)

    for n, (src, dst) in enumerate([(spn, pt), (sln, lt), (sun, ut)]):
        loads[4 + n].wait()
        for v in range(NV):
            dst[pl.ds(v, LANES, stride=8)] = src[pl.ds(128 * v, 128)].T

    def at_j(j):
        return pl.ds(pl.multiple_of(8 * j, 8), NV)

    ones5 = jnp.ones((NV, LANES), F32)
    zeros5 = jnp.zeros((NV, LANES), F32)

    def gains_ahead(j, held):
        g, p = held
        g = -(lt[at_j(j)] * g)
        gain[at_j(j)] = g
        pre[at_j(j)] = p
        return (g, -(ut[at_j(j)] * p))

    g_end, _ = lax.fori_loop(0, LANES, gains_ahead, (ones5, ones5), unroll=8)

    def gains_back(n, held):
        suf, b, c, a, low_next = held
        j = LANES - 1 - n
        l, u, p = lt[at_j(j)], ut[at_j(j)], pt[at_j(j)]
        alp[at_j(j)] = suf * p
        b = pre[at_j(j)] - low_next * b
        bet[at_j(j)] = b * p
        c = -(u * c)
        cc[at_j(j)] = c
        a = gain[at_j(j)] - u * a
        aa[at_j(j)] = a
        return (-(l * suf), b, c, a, l)

    _, _, c_top, a_top, _ = lax.fori_loop(
        0, LANES, gains_back, (ones5, zeros5, ones5, zeros5, zeros5), unroll=8
    )
    gsend[pl.ds(0, NV), 0] = g_end
    gsend[pl.ds(NV, NV), 0] = a_top
    gsend[pl.ds(2 * NV, NV), 0] = c_top
    spread(gsend, grecv, 3 * NV, 2)

    settle(recv1, (CHORD - 1) * GROUPS, 1)

    def unpack(q, _):
        for g in range(GROUPS):
            tile = recv1[pl.ds(8 * GROUPS * q + g, 8, stride=GROUPS), 0]
            for s in range(8):
                value = 8 * g + s
                if value < 85:
                    moved = tile if s == 0 else pltpu.roll(tile, LANES - 16 * s, 1)
                    expand[pl.ds(pl.multiple_of(CHORD * value + 8 * q, 8), 8)] = moved
        return 0

    lax.fori_loop(0, CHORD // 8, unpack, 0)

    def row(value, at):
        return expand[pl.ds(CHORD * value + at, 1)]

    def relay_ahead(at, held):
        new = []
        for c in range(NV):
            entry[pl.ds(CHORD * c + at, 1)] = held[c]
        for r in range(NV):
            new.append(dot([row(MAT + 5 * r + c, at) for c in range(NV)], held) + row(VEC + r, at))
        return tuple(new)

    nothing = tuple(jnp.zeros((1, LANES), F32) for _ in range(NV))
    lax.fori_loop(0, CHORD, relay_ahead, nothing, unroll=4)

    for q in range(CHORD // 8):
        vec = [entry[pl.ds(CHORD * c + 8 * q, 8)] for c in range(NV)]
        for r in range(NV):
            mats_r = [expand[pl.ds(CHORD * (INN + 5 * r + c) + 8 * q, 8)] for c in range(NV)]
            total[pl.ds(CHORD * r + 8 * q, 8)] = -(dot(mats_r, vec) + expand[pl.ds(CHORD * (SRC + r) + 8 * q, 8)])

    def relay_back(n, held):
        at = CHORD - 1 - n
        new = []
        for c in range(NV):
            entry[pl.ds(CHORD * (NV + c) + at, 1)] = held[c]
        for r in range(NV):
            new.append(
                dot([row(OUT + 5 * r + c, at) for c in range(NV)], held) + total[pl.ds(CHORD * r + at, 1)]
            )
        return tuple(new)

    lax.fori_loop(0, CHORD, relay_back, nothing, unroll=4)

    for q in range(CHORD // 8):
        for kind in range(2):
            tile = zero
            for s in range(NV):
                part_s = entry[pl.ds(CHORD * (NV * kind + s) + 8 * q, 8)]
                if s > 0:
                    part_s = pltpu.roll(part_s, 16 * s, 1)
                tile = jnp.where(blk == s, part_s, tile)
            send2[pl.ds(16 * q + kind, 8, stride=2), 0] = tile

    exchange(send2, recv2, 2, CHORD, me_c, "chord", 1)
    settle(recv2, (CHORD - 1) * 2, 3)

    for kind in range(2):
        for k in range(NK):
            tile = recv2[pl.ds(16 * k + kind, 8, stride=2), 0]
            unsh[pl.ds(8 * (NK * kind + k), 8)] = block_transpose(tile, sub, blk)
    a0 = [unsh[pl.ds(v, NK, stride=8)] for v in range(NV)]
    c1 = [unsh[pl.ds(8 * NK + v, NK, stride=8)] for v in range(NV)]
    a1 = [m + half(VEC + r, 0) for r, m in enumerate(matvec(half_matrix(MAT, 0), a0))]
    back = matvec(half_matrix(OUT, 1), c1)
    fore = matvec(half_matrix(INN, 1), a1)
    c0 = [back[r] - (fore[r] + half(SRC + r, 1)) for r in range(NV)]
    for v in range(NV):
        carry[pl.ds(8 * v, NK, stride=2)] = a0[v]
        carry[pl.ds(8 * v + 1, NK, stride=2)] = a1[v]
        carry[pl.ds(8 * (NV + v), NK, stride=2)] = c0[v]
        carry[pl.ds(8 * (NV + v) + 1, NK, stride=2)] = c1[v]

    def sweep_ahead(step, held):
        new = []
        for r in range(NV):
            at = pl.ds(pl.multiple_of((step * NV + r) * 8, 8), 8)
            val = source[at] - dot([block(lowf, 5 * r + c, step) for c in range(NV)], held)
            ysweep[at] = val
            new.append(val)
        return tuple(new)

    lax.fori_loop(0, HALF, sweep_ahead, tuple(carry[tile_of(v)] for v in range(NV)), unroll=4)

    def sweep_back(n, held):
        step = HALF - 1 - n
        new = []
        for r in range(NV):
            at = pl.ds(pl.multiple_of((step * NV + r) * 8, 8), 8)
            val = ysweep[at] - dot([block(uppf, 5 * r + c, step) for c in range(NV)], held)
            wnat[pl.ds(128 * r + step, 8, stride=HALF)] = val
            new.append(val)
        return tuple(new)

    lax.fori_loop(0, HALF, sweep_back, tuple(carry[tile_of(NV + v)] for v in range(NV)), unroll=4)

    for v in range(NV):
        wt[pl.ds(v, LANES, stride=8)] = wnat[pl.ds(128 * v, 128)].T

    def ends(j, held):
        h, w0 = held
        w = wt[at_j(j)]
        return (h + alp[at_j(j)] * w, w0 + bet[at_j(j)] * w)

    h, w0 = lax.fori_loop(0, LANES, ends, (zeros5, zeros5), unroll=8)
    hsend[pl.ds(0, NV), 0] = h
    hsend[pl.ds(NV, NV), 0] = w0
    spread(hsend, hrecv, 2 * NV, 3)

    def span_ahead(j, z):
        z = pt[at_j(j)] * wt[at_j(j)] - lt[at_j(j)] * z
        wt[at_j(j)] = z
        return z

    lax.fori_loop(0, LANES, span_ahead, zeros5, unroll=8)

    def span_back(n, z):
        j = LANES - 1 - n
        z = wt[at_j(j)] - ut[at_j(j)] * z
        wt[at_j(j)] = z
        return z

    lax.fori_loop(0, LANES, span_back, zeros5, unroll=8)

    settle(grecv, (SPAN - 1) * 3 * NV, 5)
    settle(hrecv, (SPAN - 1) * 2 * NV, 7)
    a = zeros5
    sent = []
    for d in range(SPAN):
        sentry[pl.ds(8 * d, NV)] = a
        sent.append(a)
        a = hrecv[pl.ds(2 * NV * d, NV), 0] + grecv[pl.ds(3 * NV * d, NV), 0] * a
    c = zeros5
    for d in reversed(range(SPAN)):
        sentry[pl.ds(8 * (SPAN + d), NV)] = c
        c = (
            hrecv[pl.ds(2 * NV * d + NV, NV), 0]
            + grecv[pl.ds(3 * NV * d + NV, NV), 0] * sent[d]
            + grecv[pl.ds(3 * NV * d + 2 * NV, NV), 0] * c
        )
    a_in = sentry[pl.ds(pl.multiple_of(8 * me_s, 8), NV)]
    c_in = sentry[pl.ds(pl.multiple_of(8 * (SPAN + me_s), 8), NV)]

    def close(j, _):
        wt[at_j(j)] = wt[at_j(j)] + aa[at_j(j)] * a_in + cc[at_j(j)] * c_in
        return 0

    lax.fori_loop(0, LANES, close, 0, unroll=8)

    for n in range(7, 10):
        loads[n].wait()
    for v in range(NV):
        x = wt[pl.ds(v, LANES, stride=8)].T
        held = None
        planes = []
        for k in range(NK):
            at = pl.ds(128 * v + 32 * k, 32)
            now = npn[at].astype(F32) * x[32 * k : 32 * k + 32]
            held = now if held is None else now - nln[at].astype(F32) * held
            planes.append(held)
        held = None
        for k in reversed(range(NK)):
            at = pl.ds(128 * v + 32 * k, 32)
            held = planes[k] if held is None else planes[k] - nun[at].astype(F32) * held
            out_ref[at] = held

    settle(send1, (CHORD - 1) * GROUPS, 0)
    settle(send2, (CHORD - 1) * 2, 2)
    settle(grecv, (SPAN - 1) * 3 * NV, 4)
    settle(hrecv, (SPAN - 1) * 2 * NV, 6)


def on_device(*args):
    flat = [a.reshape(-1, LANES) for a in args]
    f32 = lambda *shape: pltpu.VMEM(shape, F32)
    b16 = lambda *shape: pltpu.VMEM(shape, jnp.bfloat16)
    wide, narrow = NV * NV * 128, NV * 128
    scratch = [
        f32(narrow, LANES), b16(wide, LANES), b16(wide, LANES), b16(wide, LANES),
        f32(narrow, LANES), f32(narrow, LANES), f32(narrow, LANES),
        b16(narrow, LANES), b16(narrow, LANES), b16(narrow, LANES),
        f32(wide, LANES), f32(wide, LANES), f32(wide, LANES),
        f32(HALF * NV * 8, LANES),
        f32(88 * 8, LANES),
        f32(88 * NK, LANES),
        f32(CHORD * GROUPS, 1, LANES), f32(CHORD * GROUPS, 1, LANES),
        f32(88 * CHORD, LANES),
        f32(2 * NV * CHORD, LANES), f32(NV * CHORD, LANES),
        f32(2 * CHORD, 1, LANES), f32(2 * CHORD, 1, LANES),
        f32(64, LANES), f32(80, LANES),
        f32(HALF * NV * 8, LANES), f32(narrow, LANES),
    ]
    scratch += [f32(8 * LANES, LANES) for _ in range(10)]
    scratch += [
        f32(3 * NV, 1, LANES), f32(SPAN * 3 * NV, 1, LANES),
        f32(2 * NV, 1, LANES), f32(SPAN * 2 * NV, 1, LANES),
        f32(2 * SPAN * 8, LANES),
        pltpu.SemaphoreType.DMA((10,)),
        pltpu.SemaphoreType.DMA((8,)),
    ]
    out = pl.pallas_call(
        kernel,
        out_shape=jax.ShapeDtypeStruct((narrow, LANES), F32),
        in_specs=[pl.BlockSpec(memory_space=pl.ANY)] * 10,
        out_specs=pl.BlockSpec(memory_space=pltpu.VMEM),
        scratch_shapes=scratch,
        compiler_params=pltpu.CompilerParams(
            collective_id=0, has_side_effects=True, vmem_limit_bytes=40 * 1024 * 1024
        ),
    )(*flat)
    return out.reshape(NV, NK, CELLS, LANES)


def solution(mesh):
    grid = P(None, None, "chord", "span")
    deep = P(None, None, None, "chord", "span")
    return jax.shard_map(
        on_device,
        mesh=mesh,
        in_specs=(grid, deep, deep, deep, grid, grid, grid, grid, grid, grid),
        out_specs=grid,
        check_vma=False,
    )
```

time: 749 us -> 47.5 us (0.06)
  the two profiles are of different devices: /device:TPU:102 before, /device:TPU:1 now
where the time goes in v1:
time: 47.5 us; the launch traced here: 47.1 us
  Pallas kernels  36.3 us (76%)
  local copies, waits for them, and re-layouts  10.8 us (23%)
    pallas_call x1, Pallas kernels, on_device(): pl.pallas_call(kernel, out_shape=jax.ShapeDtypeStruct((narrow, LANES), F3...  36.3 us
    unnamed x21, local copies, waits for them, and re-layouts  10.8 us

profile of v1, /device:TPU:1, one launch (start us, length us, event | category | flops | bytes accessed | tf_op | source)
XLA Modules:
  0.0 47.1 jit_solution(9170890616595968922)
XLA Ops:
  0.0 0.0 copy-start
  0.0 1.1 %copy-done = bf16[5,5,4,32,128]{4,3,2,1,0:T(8,128)(2,1)S(1)} copy-done((bf16[5,5,4,32,128]{4,3,2,1,0:T(8,128)(2,1)S(1)}, bf16[5,5,4,32,128]{4,3,2,1,0:T(8,128)(2,1)}, u32[]{:S(2)}) %copy-start) | copy-done | bytes 819224
  1.1 0.0 copy-start.1
  1.1 1.1 %copy-done.1 = bf16[5,5,4,32,128]{4,3,2,1,0:T(8,128)(2,1)S(1)} copy-done((bf16[5,5,4,32,128]{4,3,2,1,0:T(8,128)(2,1)S(1)}, bf16[5,5,4,32,128]{4,3,2,1,0:T(8,128)(2,1)}, u32[]{:S(2)}) %copy-start.1) | copy-done | bytes 819224
  2.3 0.0 copy-start.2
  2.3 1.1 %copy-done.2 = bf16[5,5,4,32,128]{4,3,2,1,0:T(8,128)(2,1)S(1)} copy-done((bf16[5,5,4,32,128]{4,3,2,1,0:T(8,128)(2,1)S(1)}, bf16[5,5,4,32,128]{4,3,2,1,0:T(8,128)(2,1)}, u32[]{:S(2)}) %copy-start.2) | copy-done | bytes 819224
  3.4 0.0 copy-start.3
  3.4 1.0 %copy-done.3 = f32[5,4,32,128]{3,2,1,0:T(8,128)S(1)} copy-done((f32[5,4,32,128]{3,2,1,0:T(8,128)S(1)}, f32[5,4,32,128]{3,2,1,0:T(8,128)}, u32[]{:S(2)}) %copy-start.3) | copy-done | bytes 327704
  4.4 0.0 copy-start.4
  4.4 1.0 %copy-done.4 = f32[5,4,32,128]{3,2,1,0:T(8,128)S(1)} copy-done((f32[5,4,32,128]{3,2,1,0:T(8,128)S(1)}, f32[5,4,32,128]{3,2,1,0:T(8,128)}, u32[]{:S(2)}) %copy-start.4) | copy-done | bytes 327704
  5.4 0.0 copy-start.5
  5.4 1.0 %copy-done.5 = f32[5,4,32,128]{3,2,1,0:T(8,128)S(1)} copy-done((f32[5,4,32,128]{3,2,1,0:T(8,128)S(1)}, f32[5,4,32,128]{3,2,1,0:T(8,128)}, u32[]{:S(2)}) %copy-start.5) | copy-done | bytes 327704
  6.4 0.0 copy-start.6
  6.4 1.0 %copy-done.6 = f32[5,4,32,128]{3,2,1,0:T(8,128)S(1)} copy-done((f32[5,4,32,128]{3,2,1,0:T(8,128)S(1)}, f32[5,4,32,128]{3,2,1,0:T(8,128)}, u32[]{:S(2)}) %copy-start.6) | copy-done | bytes 327704
  7.3 0.0 copy-start.7
  7.3 0.9 %copy-done.7 = bf16[5,4,32,128]{3,2,1,0:T(8,128)(2,1)S(1)} copy-done((bf16[5,4,32,128]{3,2,1,0:T(8,128)(2,1)S(1)}, bf16[5,4,32,128]{3,2,1,0:T(8,128)(2,1)}, u32[]{:S(2)}) %copy-start.7) | copy-done | bytes 163864
  8.2 0.0 copy-start.8
  8.2 0.9 %copy-done.8 = bf16[5,4,32,128]{3,2,1,0:T(8,128)(2,1)S(1)} copy-done((bf16[5,4,32,128]{3,2,1,0:T(8,128)(2,1)S(1)}, bf16[5,4,32,128]{3,2,1,0:T(8,128)(2,1)}, u32[]{:S(2)}) %copy-start.8) | copy-done | bytes 163864
  9.2 0.0 copy-start.9
  9.2 0.9 %copy-done.9 = bf16[5,4,32,128]{3,2,1,0:T(8,128)(2,1)S(1)} copy-done((bf16[5,4,32,128]{3,2,1,0:T(8,128)(2,1)S(1)}, bf16[5,4,32,128]{3,2,1,0:T(8,128)(2,1)}, u32[]{:S(2)}) %copy-start.9) | copy-done | bytes 163864
  10.1 36.3 %shard_map.100 = f32[640,128]{1,0:T(8,128)S(1)} custom-call(f32[640,128]{1,0:T(8,128)S(1)} %bitcast.15, bf16[3200,128]{1,0:T(8,128)(2,1)S(1)} %bitcast.12, bf16[3200,128]{1,0:T(8,128)(2,1)S(1)} %bitcast.13, bf16[3200,128]{1,0:T(8,128)(2,1)S(1)} %bitcast.14, f32[640,128]{1,0:T(8,128)S(1)} %bitcast.16, f32[640,128]{1,0:T(8,128)S(1)} %bitcast.17, ...), custom_call_target="tpu_custom_call" | custom-call | tf_op jit(solution)/shard_map/pallas_call | solution.py:493
  46.3 0.7 %copy.12 = f32[5,4,32,128]{3,2,1,0:T(8,128)} copy(f32[5,4,32,128]{3,2,1,0:T(8,128)S(1)} %bitcast.11) | data formatting | bytes 655360
Async XLA Ops:
  0.0 1.1 %copy-start = (bf16[5,5,4,32,128]{4,3,2,1,0:T(8,128)(2,1)S(1)}, bf16[5,5,4,32,128]{4,3,2,1,0:T(8,128)(2,1)}, u32[]{:S(2)}) copy-start(bf16[5,5,4,32,128]{4,3,2,1,0:T(8,128)(2,1)} %param.11) | copy-start | bytes 2457604
  1.1 1.1 %copy-start.1 = (bf16[5,5,4,32,128]{4,3,2,1,0:T(8,128)(2,1)S(1)}, bf16[5,5,4,32,128]{4,3,2,1,0:T(8,128)(2,1)}, u32[]{:S(2)}) copy-start(bf16[5,5,4,32,128]{4,3,2,1,0:T(8,128)(2,1)} %param.12) | copy-start | bytes 2457604
  2.3 1.1 %copy-start.2 = (bf16[5,5,4,32,128]{4,3,2,1,0:T(8,128)(2,1)S(1)}, bf16[5,5,4,32,128]{4,3,2,1,0:T(8,128)(2,1)}, u32[]{:S(2)}) copy-start(bf16[5,5,4,32,128]{4,3,2,1,0:T(8,128)(2,1)} %param.13) | copy-start | bytes 2457604
  3.4 1.0 %copy-start.3 = (f32[5,4,32,128]{3,2,1,0:T(8,128)S(1)}, f32[5,4,32,128]{3,2,1,0:T(8,128)}, u32[]{:S(2)}) copy-start(f32[5,4,32,128]{3,2,1,0:T(8,128)} %param.10) | copy-start | bytes 983044
  4.4 1.0 %copy-start.4 = (f32[5,4,32,128]{3,2,1,0:T(8,128)S(1)}, f32[5,4,32,128]{3,2,1,0:T(8,128)}, u32[]{:S(2)}) copy-start(f32[5,4,32,128]{3,2,1,0:T(8,128)} %param.14) | copy-start | bytes 983044
  5.4 1.0 %copy-start.5 = (f32[5,4,32,128]{3,2,1,0:T(8,128)S(1)}, f32[5,4,32,128]{3,2,1,0:T(8,128)}, u32[]{:S(2)}) copy-start(f32[5,4,32,128]{3,2,1,0:T(8,128)} %param.15) | copy-start | bytes 983044
  6.4 1.0 %copy-start.6 = (f32[5,4,32,128]{3,2,1,0:T(8,128)S(1)}, f32[5,4,32,128]{3,2,1,0:T(8,128)}, u32[]{:S(2)}) copy-start(f32[5,4,32,128]{3,2,1,0:T(8,128)} %param.16) | copy-start | bytes 983044
  7.3 0.9 %copy-start.7 = (bf16[5,4,32,128]{3,2,1,0:T(8,128)(2,1)S(1)}, bf16[5,4,32,128]{3,2,1,0:T(8,128)(2,1)}, u32[]{:S(2)}) copy-start(bf16[5,4,32,128]{3,2,1,0:T(8,128)(2,1)} %param.17) | copy-start | bytes 491524
  8.2 0.9 %copy-start.8 = (bf16[5,4,32,128]{3,2,1,0:T(8,128)(2,1)S(1)}, bf16[5,4,32,128]{3,2,1,0:T(8,128)(2,1)}, u32[]{:S(2)}) copy-start(bf16[5,4,32,128]{3,2,1,0:T(8,128)(2,1)} %param.18) | copy-start | bytes 491524
  9.2 0.9 %copy-start.9 = (bf16[5,4,32,128]{3,2,1,0:T(8,128)(2,1)S(1)}, bf16[5,4,32,128]{3,2,1,0:T(8,128)(2,1)}, u32[]{:S(2)}) copy-start(bf16[5,4,32,128]{3,2,1,0:T(8,128)(2,1)} %param.19) | copy-start | bytes 491524

commit v2 on v1

--- a/solution.py
+++ b/solution.py
@@ -19,6 +19,17 @@
 HALF = 16
 GROUPS = 11
 MAT, VEC, OUT, INN, SRC = 0, 25, 30, 55, 80
+ZS, XS = 8, 4
+
+
+def ring(step, size):
+    return min(step, size - step)
+
+
+CHORD_PEERS = sorted(
+    [(dz, dx) for dz in range(ZS) for dx in range(XS) if dz or dx], key=lambda p: -ring(p[0], ZS) - ring(p[1], XS)
+)
+SPAN_PEERS = (4, 5, 3, 2, 6, 7, 1)
 
 
 def dot(lhs, rhs):
@@ -26,6 +37,16 @@
     while len(terms) > 1:
         terms = [terms[i] + terms[i + 1] if i + 1 < len(terms) else terms[i] for i in range(0, len(terms), 2)]
     return terms[0]
+
+
+def affine(lhs, rhs, extra):
+    a, b, c, d, e = [x * y for x, y in zip(lhs, rhs)]
+    return ((a + b) + (c + d)) + (e + extra)
+
+
+def residue(extra, lhs, rhs):
+    a, b, c, d, e = [x * y for x, y in zip(lhs, rhs)]
+    return (extra - e) - ((a + b) + (c + d))
 
 
 def column(matrix, index):
@@ -63,32 +84,31 @@
     send2, recv2, unsh, carry, ysweep, wnat,
     wt, pt, lt, ut, gain, pre, alp, bet, cc, aa,
     gsend, grecv, hsend, hrecv, sentry,
+    lows_by, upps_by, wvar, alp_v, bet_v,
     load_sem, sems,
 ):
     me_c = lax.axis_index("chord")
     me_s = lax.axis_index("span")
 
-    loads = []
-    for n, (src, dst) in enumerate(
-        [(res_h, res), (piv_h, piv), (low_h, low), (upp_h, upp), (sp_h, spn), (sl_h, sln), (su_h, sun),
-         (np_h, npn), (nl_h, nln), (nu_h, nun)]
-    ):
+    z, x = me_c // XS, lax.rem(me_c, XS)
+
+    def chord_peer(peer):
+        return lax.rem(z + peer[0], ZS) * XS + lax.rem(x + peer[1], XS)
+
+    barrier = pltpu.get_barrier_semaphore()
+    for peer in CHORD_PEERS:
+        pl.semaphore_signal(barrier, inc=1, device_id={"chord": chord_peer(peer)}, device_id_type=MESH)
+    for o in SPAN_PEERS:
+        pl.semaphore_signal(barrier, inc=1, device_id={"span": lax.rem(me_s + o, SPAN)}, device_id_type=MESH)
+
+    loads = {}
+    for n, src, dst in [
+        (1, piv_h, piv), (0, res_h, res), (2, low_h, low), (3, upp_h, upp), (4, sp_h, spn), (5, sl_h, sln),
+        (6, su_h, sun), (7, np_h, npn), (8, nl_h, nln), (9, nu_h, nun),
+    ]:
         copy = pltpu.make_async_copy(src, dst, load_sem.at[n])
         copy.start()
-        loads.append(copy)
-
-    barrier = pltpu.get_barrier_semaphore()
-
-    def greet_chord(o, _):
-        pl.semaphore_signal(barrier, inc=1, device_id={"chord": lax.rem(me_c + o, CHORD)}, device_id_type=MESH)
-        return 0
-
-    def greet_span(o, _):
-        pl.semaphore_signal(barrier, inc=1, device_id={"span": lax.rem(me_s + o, SPAN)}, device_id_type=MESH)
-        return 0
-
-    lax.fori_loop(1, CHORD, greet_chord, 0)
-    lax.fori_loop(1, SPAN, greet_span, 0)
+        loads[n] = copy
 
     sub = lax.broadcasted_iota(jnp.int32, (8, LANES), 0)
     lane = lax.broadcasted_iota(jnp.int32, (8, LANES), 1)
@@ -209,24 +229,21 @@
 
     pl.semaphore_wait(barrier, CHORD - 1 + SPAN - 1)
 
-    def exchange(send, recv, rows, count, me, axis, at):
-        def start(o, _):
-            to = lax.rem(me + o, count)
+    def exchange(send, recv, rows, at):
+        for peer in CHORD_PEERS:
+            to = chord_peer(peer)
             pltpu.make_async_remote_copy(
                 src_ref=send.at[pl.ds(to * rows, rows)],
-                dst_ref=recv.at[pl.ds(me * rows, rows)],
+                dst_ref=recv.at[pl.ds(me_c * rows, rows)],
                 send_sem=sems.at[2 * at],
                 recv_sem=sems.at[2 * at + 1],
-                device_id={axis: to},
+                device_id={"chord": to},
                 device_id_type=MESH,
             ).start()
-            return 0
-
-        lax.fori_loop(1, count, start, 0)
-        recv[pl.ds(me * rows, rows)] = send[pl.ds(me * rows, rows)]
+        recv[pl.ds(me_c * rows, rows)] = send[pl.ds(me_c * rows, rows)]
 
     def spread(send, recv, rows, at):
-        def start(o, _):
+        for o in SPAN_PEERS:
             pltpu.make_async_remote_copy(
                 src_ref=send,
                 dst_ref=recv.at[pl.ds(me_s * rows, rows)],
@@ -235,16 +252,13 @@
                 device_id={"span": lax.rem(me_s + o, SPAN)},
                 device_id_type=MESH,
             ).start()
-            return 0
-
-        lax.fori_loop(1, SPAN, start, 0)
         recv[pl.ds(me_s * rows, rows)] = send[...]
 
     def settle(ref, rows, sem):
         whole = ref.at[pl.ds(0, rows)]
         pltpu.make_async_copy(whole, whole, sems.at[sem]).wait()
 
-    exchange(send1, recv1, GROUPS, CHORD, me_c, "chord", 0)
+    exchange(send1, recv1, GROUPS, 0)
 
     for n, (src, dst) in enumerate([(spn, pt), (sln, lt), (sun, ut)]):
         loads[4 + n].wait()
@@ -286,6 +300,9 @@
     gsend[pl.ds(NV, NV), 0] = a_top
     gsend[pl.ds(2 * NV, NV), 0] = c_top
     spread(gsend, grecv, 3 * NV, 2)
+    for v in range(NV):
+        alp_v[pl.ds(128 * v, 128)] = alp[pl.ds(v, LANES, stride=8)]
+        bet_v[pl.ds(128 * v, 128)] = bet[pl.ds(v, LANES, stride=8)]
 
     settle(recv1, (CHORD - 1) * GROUPS, 1)
 
@@ -309,7 +326,7 @@
         for c in range(NV):
             entry[pl.ds(CHORD * c + at, 1)] = held[c]
         for r in range(NV):
-            new.append(dot([row(MAT + 5 * r + c, at) for c in range(NV)], held) + row(VEC + r, at))
+            new.append(affine([row(MAT + 5 * r + c, at) for c in range(NV)], held, row(VEC + r, at)))
         return tuple(new)
 
     nothing = tuple(jnp.zeros((1, LANES), F32) for _ in range(NV))
@@ -328,7 +345,7 @@
             entry[pl.ds(CHORD * (NV + c) + at, 1)] = held[c]
         for r in range(NV):
             new.append(
-                dot([row(OUT + 5 * r + c, at) for c in range(NV)], held) + total[pl.ds(CHORD * r + at, 1)]
+                affine([row(OUT + 5 * r + c, at) for c in range(NV)], held, total[pl.ds(CHORD * r + at, 1)])
             )
         return tuple(new)
 
@@ -344,7 +361,16 @@
                 tile = jnp.where(blk == s, part_s, tile)
             send2[pl.ds(16 * q + kind, 8, stride=2), 0] = tile
 
-    exchange(send2, recv2, 2, CHORD, me_c, "chord", 1)
+    exchange(send2, recv2, 2, 1)
+
+    def gather_steps(step, _):
+        for index in range(NV * NV):
+            at = pl.ds(pl.multiple_of((step * NV * NV + index) * 8, 8), 8)
+            lows_by[at] = block(lowf, index, step)
+            upps_by[at] = block(uppf, index, step)
+        return 0
+
+    lax.fori_loop(0, HALF, gather_steps, 0)
     settle(recv2, (CHORD - 1) * 2, 3)
 
     for kind in range(2):
@@ -363,11 +389,14 @@
         carry[pl.ds(8 * (NV + v), NK, stride=2)] = c0[v]
         carry[pl.ds(8 * (NV + v) + 1, NK, stride=2)] = c1[v]
 
+    def by_step(ref, step, r):
+        return [ref[pl.ds(pl.multiple_of((step * NV * NV + NV * r + c) * 8, 8), 8)] for c in range(NV)]
+
     def sweep_ahead(step, held):
         new = []
         for r in range(NV):
             at = pl.ds(pl.multiple_of((step * NV + r) * 8, 8), 8)
-            val = source[at] - dot([block(lowf, 5 * r + c, step) for c in range(NV)], held)
+            val = residue(source[at], by_step(lows_by, step, r), held)
             ysweep[at] = val
             new.append(val)
         return tuple(new)
@@ -379,7 +408,7 @@
         new = []
         for r in range(NV):
             at = pl.ds(pl.multiple_of((step * NV + r) * 8, 8), 8)
-            val = ysweep[at] - dot([block(uppf, 5 * r + c, step) for c in range(NV)], held)
+            val = residue(ysweep[at], by_step(upps_by, step, r), held)
             wnat[pl.ds(128 * r + step, 8, stride=HALF)] = val
             new.append(val)
         return tuple(new)
@@ -387,17 +416,16 @@
     lax.fori_loop(0, HALF, sweep_back, tuple(carry[tile_of(NV + v)] for v in range(NV)), unroll=4)
 
     for v in range(NV):
-        wt[pl.ds(v, LANES, stride=8)] = wnat[pl.ds(128 * v, 128)].T
-
-    def ends(j, held):
-        h, w0 = held
-        w = wt[at_j(j)]
-        return (h + alp[at_j(j)] * w, w0 + bet[at_j(j)] * w)
-
-    h, w0 = lax.fori_loop(0, LANES, ends, (zeros5, zeros5), unroll=8)
-    hsend[pl.ds(0, NV), 0] = h
-    hsend[pl.ds(NV, NV), 0] = w0
+        turned = wnat[pl.ds(128 * v, 128)].T
+        wvar[pl.ds(128 * v, 128)] = turned
+        for kind, weight in enumerate((alp_v, bet_v)):
+            terms = [turned[8 * t : 8 * t + 8] * weight[pl.ds(128 * v + 8 * t, 8)] for t in range(16)]
+            while len(terms) > 1:
+                terms = [terms[t] + terms[t + 1] for t in range(0, len(terms), 2)]
+            hsend[pl.ds(NV * kind + v, 1), 0] = jnp.sum(terms[0], axis=0, keepdims=True)
     spread(hsend, hrecv, 2 * NV, 3)
+    for v in range(NV):
+        wt[pl.ds(v, LANES, stride=8)] = wvar[pl.ds(128 * v, 128)]
 
     def span_ahead(j, z):
         z = pt[at_j(j)] * wt[at_j(j)] - lt[at_j(j)] * z
@@ -487,6 +515,7 @@
         f32(3 * NV, 1, LANES), f32(SPAN * 3 * NV, 1, LANES),
         f32(2 * NV, 1, LANES), f32(SPAN * 2 * NV, 1, LANES),
         f32(2 * SPAN * 8, LANES),
+        f32(wide, LANES), f32(wide, LANES), f32(narrow, LANES), f32(narrow, LANES), f32(narrow, LANES),
         pltpu.SemaphoreType.DMA((10,)),
         pltpu.SemaphoreType.DMA((8,)),
     ]
@@ -497,7 +526,7 @@
         out_specs=pl.BlockSpec(memory_space=pltpu.VMEM),
         scratch_shapes=scratch,
         compiler_params=pltpu.CompilerParams(
-            collective_id=0, has_side_effects=True, vmem_limit_bytes=40 * 1024 * 1024
+            collective_id=0, has_side_effects=True, vmem_limit_bytes=60 * 1024 * 1024
         ),
     )(*flat)
     return out.reshape(NV, NK, CELLS, LANES)

time: 47.5 us -> 36.4 us (0.77)
  local copies, waits for them, and re-layouts: 10.8 us -> 1.72 us
  Pallas kernels: 36.3 us -> 34.6 us
    unnamed x21 -> x1, local copies, waits for them, and re-layouts: 10.8 us -> 1.72 us
    pallas_call x1, Pallas kernels: 36.3 us -> 34.6 us  [on_device(): pl.pallas_call(kernel, out_shape=jax.ShapeDtypeStruct((narrow, LANES), F3...]
where the time goes in v2:
time: 36.4 us; the launch traced here: 36.3 us
  Pallas kernels  34.6 us (95%)
  local copies, waits for them, and re-layouts  1.72 us (5%)
    pallas_call x1, Pallas kernels, on_device(): pl.pallas_call(kernel, out_shape=jax.ShapeDtypeStruct((narrow, LANES), F3...  34.6 us
    unnamed x1, local copies, waits for them, and re-layouts  1.72 us

profile of v2, /device:TPU:1, one launch (start us, length us, event | category | flops | bytes accessed | tf_op | source)
XLA Modules:
  0.0 36.3 jit_solution(18233611907396876768)
XLA Ops:
  0.0 34.6 %shard_map.100 = f32[640,128]{1,0:T(8,128)} custom-call(f32[640,128]{1,0:T(8,128)} %bitcast.15, bf16[3200,128]{1,0:T(8,128)(2,1)} %bitcast.12, bf16[3200,128]{1,0:T(8,128)(2,1)} %bitcast.13, bf16[3200,128]{1,0:T(8,128)(2,1)} %bitcast.14, f32[640,128]{1,0:T(8,128)} %bitcast.16, f32[640,128]{1,0:T(8,128)} %bitcast.17, f32[640,128]{1,0:T(8,128)} %bitcast.18, ...), custom_call_target="tpu_custom_call" | custom-call | tf_op jit(solution)/shard_map/pallas_call | solution.py:522
  34.6 1.7 %copy.12 = f32[5,4,32,128]{3,2,1,0:T(8,128)} copy(f32[5,4,32,128]{3,2,1,0:T(8,128)} %bitcast.11) | data formatting | bytes 655360

commit v3 on v2

--- a/solution.py
+++ b/solution.py
@@ -80,11 +80,11 @@
     res_h, piv_h, low_h, upp_h, sp_h, sl_h, su_h, np_h, nl_h, nu_h,
     out_ref,
     res, piv, low, upp, spn, sln, sun, npn, nln, nun,
-    pivf, lowf, uppf, source, state, comb, send1, recv1, expand, entry, total,
+    pivf, lowf, uppf, source, state, comb, send1, recv1, expand, expand2, entry, entry2, total,
     send2, recv2, unsh, carry, ysweep, wnat,
     wt, pt, lt, ut, gain, pre, alp, bet, cc, aa,
     gsend, grecv, hsend, hrecv, sentry,
-    lows_by, upps_by, wvar, alp_v, bet_v,
+    wvar, alp_v, bet_v,
     load_sem, sems,
 ):
     me_c = lax.axis_index("chord")
@@ -114,13 +114,17 @@
     lane = lax.broadcasted_iota(jnp.int32, (8, LANES), 1)
     blk = lane // 16
 
+    to_row = lax.broadcasted_iota(jnp.int32, (LANES, LANES), 0)
+    from_row = lax.broadcasted_iota(jnp.int32, (LANES, LANES), 1)
+    order = jnp.where(from_row == HALF * lax.rem(to_row, 8) + to_row // 8, 1.0, 0.0).astype(jnp.bfloat16)
+
     def widen(src, dst):
         def body(n, _):
             rows = pl.ds(pl.multiple_of(n * 128, 128), 128)
-            dst[rows] = src[rows].astype(F32)
+            dst[rows] = jnp.dot(order, src[rows], preferred_element_type=F32)
             return 0
 
-        lax.fori_loop(0, NV * NV, body, 0)
+        lax.fori_loop(0, NV * NV, body, 0, unroll=5)
 
     loads[1].wait()
     widen(piv, pivf)
@@ -131,57 +135,68 @@
     loads[0].wait()
 
     zero = jnp.zeros((8, LANES), F32)
-    one = jnp.ones((8, LANES), F32)
 
     def tile_of(value):
         return pl.ds(8 * value, 8)
 
+    def strided(ref, index, step):
+        return ref[pl.ds(index * 128 + step, 8, stride=HALF)]
+
+    def block(ref, index, step):
+        return ref[pl.ds(pl.multiple_of(index * 128 + 8 * step, 8), 8)]
+
+    def blocks(ref, step):
+        return [[block(ref, 5 * r + c, step) for c in range(NV)] for r in range(NV)]
+
+    def sources(step):
+        cells = [strided(res, c, step) for c in range(NV)]
+        src = [dot([block(pivf, 5 * r + c, step) for c in range(NV)], cells) for r in range(NV)]
+        for r in range(NV):
+            source[pl.ds(pl.multiple_of((step * NV + r) * 8, 8), 8)] = src[r]
+        return src
+
+    def map_step(step, odd):
+        src = sources(step)
+        lows = blocks(lowf, step)
+        cols = []
+        for c in range(NV):
+            new = matvec(lows, [state[tile_of(MAT + 5 * r + c)] for r in range(NV)])
+            for r in range(NV):
+                state[tile_of(MAT + 5 * r + c)] = new[r]
+            cols.append(new)
+        vec = [state[tile_of(VEC + r)] for r in range(NV)]
+        new = [affine(lows[r], vec, src[r]) if odd else -residue(src[r], lows[r], vec) for r in range(NV)]
+        for r in range(NV):
+            state[tile_of(VEC + r)] = new[r]
+        cols.append(new)
+        upps = blocks(uppf, step)
+        for r in range(NV):
+            row = [state[tile_of(OUT + 5 * r + c)] for c in range(NV)]
+            for c in range(NV):
+                at = tile_of(INN + 5 * r + c)
+                state[at] = affine(row, cols[c], state[at])
+            at = tile_of(SRC + r)
+            state[at] = affine(row, cols[NV], state[at])
+            for c in range(NV):
+                state[tile_of(OUT + 5 * r + c)] = dot(row, column(upps, c))
+
+    first = sources(0)
     for r in range(NV):
         for c in range(NV):
-            state[tile_of(MAT + 5 * r + c)] = one if r == c else zero
-            state[tile_of(OUT + 5 * r + c)] = one if r == c else zero
-            state[tile_of(INN + 5 * r + c)] = zero
-        state[tile_of(VEC + r)] = zero
-        state[tile_of(SRC + r)] = zero
-
-    def block(ref, index, step):
-        return ref[pl.ds(index * 128 + step, 8, stride=HALF)]
-
-    def blocks(ref, step):
-        return [[block(ref, 5 * r + c, step) for c in range(NV)] for r in range(NV)]
-
-    def map_step(pair, _):
-        for odd in range(2):
-            step = 2 * pair + odd
-            cells = [block(res, c, step) for c in range(NV)]
-            src = [dot([block(pivf, 5 * r + c, step) for c in range(NV)], cells) for r in range(NV)]
-            for r in range(NV):
-                source[pl.ds(pl.multiple_of((step * NV + r) * 8, 8), 8)] = src[r]
-            lows = blocks(lowf, step)
-            cols = []
-            for c in range(NV):
-                new = matvec(lows, [state[tile_of(MAT + 5 * r + c)] for r in range(NV)])
-                for r in range(NV):
-                    state[tile_of(MAT + 5 * r + c)] = new[r]
-                cols.append(new)
-            new = matvec(lows, [state[tile_of(VEC + r)] for r in range(NV)])
-            new = [n + s if odd else n - s for n, s in zip(new, src)]
-            for r in range(NV):
-                state[tile_of(VEC + r)] = new[r]
-            cols.append(new)
-            upps = blocks(uppf, step)
-            for r in range(NV):
-                row = [state[tile_of(OUT + 5 * r + c)] for c in range(NV)]
-                for c in range(NV):
-                    at = tile_of(INN + 5 * r + c)
-                    state[at] = state[at] + dot(row, cols[c])
-                at = tile_of(SRC + r)
-                state[at] = state[at] + dot(row, cols[NV])
-                for c in range(NV):
-                    state[tile_of(OUT + 5 * r + c)] = dot(row, column(upps, c))
+            low = block(lowf, 5 * r + c, 0)
+            state[tile_of(MAT + 5 * r + c)] = low
+            state[tile_of(INN + 5 * r + c)] = low
+            state[tile_of(OUT + 5 * r + c)] = block(uppf, 5 * r + c, 0)
+        state[tile_of(VEC + r)] = -first[r]
+        state[tile_of(SRC + r)] = -first[r]
+    map_step(1, True)
+
+    def map_pair(pair, _):
+        map_step(2 * pair, False)
+        map_step(2 * pair + 1, True)
         return 0
 
-    lax.fori_loop(0, HALF // 2, map_step, 0)
+    lax.fori_loop(1, HALF // 2, map_pair, 0)
 
     def half(value, which):
         return state[pl.ds(8 * value + which, NK, stride=2)]
@@ -306,56 +321,75 @@
 
     settle(recv1, (CHORD - 1) * GROUPS, 1)
 
-    def unpack(q, _):
-        for g in range(GROUPS):
+    ahead_values = 8 * (OUT // 8 + 1)
+
+    def unpack(q, groups):
+        for g in groups:
             tile = recv1[pl.ds(8 * GROUPS * q + g, 8, stride=GROUPS), 0]
             for s in range(8):
                 value = 8 * g + s
                 if value < 85:
                     moved = tile if s == 0 else pltpu.roll(tile, LANES - 16 * s, 1)
-                    expand[pl.ds(pl.multiple_of(CHORD * value + 8 * q, 8), 8)] = moved
-        return 0
-
-    lax.fori_loop(0, CHORD // 8, unpack, 0)
+                    if value < ahead_values:
+                        expand[pl.ds(pl.multiple_of(CHORD * value + 8 * q, 8), 8)] = moved
+                    if value >= OUT:
+                        expand2[pl.ds(pl.multiple_of(CHORD * (value - OUT) + 8 * q, 8), 8)] = moved
 
     def row(value, at):
         return expand[pl.ds(CHORD * value + at, 1)]
 
-    def relay_ahead(at, held):
-        new = []
-        for c in range(NV):
-            entry[pl.ds(CHORD * c + at, 1)] = held[c]
-        for r in range(NV):
-            new.append(affine([row(MAT + 5 * r + c, at) for c in range(NV)], held, row(VEC + r, at)))
-        return tuple(new)
-
-    nothing = tuple(jnp.zeros((1, LANES), F32) for _ in range(NV))
-    lax.fori_loop(0, CHORD, relay_ahead, nothing, unroll=4)
+    def row2(value, at):
+        return expand2[pl.ds(CHORD * (value - OUT) + at, 1)]
+
+    def tile2(value, q):
+        return expand2[pl.ds(pl.multiple_of(CHORD * (value - OUT) + 8 * q, 8), 8)]
+
+    def relay_ahead(q, held):
+        for n in range(8):
+            at = 8 * q + n
+            new = []
+            for c in range(NV):
+                entry[pl.ds(CHORD * c + at, 1)] = held[c]
+            for r in range(NV):
+                new.append(affine([row(MAT + 5 * r + c, at) for c in range(NV)], held, row(VEC + r, at)))
+            held = new
+        return held
+
+    held = [jnp.zeros((1, LANES), F32) for _ in range(NV)]
+    for q in range(CHORD // 8):
+        unpack(q, range(ahead_values // 8))
+    for q in range(CHORD // 8):
+        held = relay_ahead(q, held)
+        unpack(q, range(ahead_values // 8, GROUPS))
 
     for q in range(CHORD // 8):
         vec = [entry[pl.ds(CHORD * c + 8 * q, 8)] for c in range(NV)]
         for r in range(NV):
-            mats_r = [expand[pl.ds(CHORD * (INN + 5 * r + c) + 8 * q, 8)] for c in range(NV)]
-            total[pl.ds(CHORD * r + 8 * q, 8)] = -(dot(mats_r, vec) + expand[pl.ds(CHORD * (SRC + r) + 8 * q, 8)])
-
-    def relay_back(n, held):
-        at = CHORD - 1 - n
-        new = []
-        for c in range(NV):
-            entry[pl.ds(CHORD * (NV + c) + at, 1)] = held[c]
-        for r in range(NV):
-            new.append(
-                affine([row(OUT + 5 * r + c, at) for c in range(NV)], held, total[pl.ds(CHORD * r + at, 1)])
-            )
-        return tuple(new)
-
-    lax.fori_loop(0, CHORD, relay_back, nothing, unroll=4)
+            mats_r = [tile2(INN + 5 * r + c, q) for c in range(NV)]
+            total[pl.ds(CHORD * r + 8 * q, 8)] = -affine(mats_r, vec, tile2(SRC + r, q))
+
+    def relay_back(q, held):
+        for n in reversed(range(8)):
+            at = 8 * q + n
+            new = []
+            for c in range(NV):
+                entry2[pl.ds(CHORD * c + at, 1)] = held[c]
+            for r in range(NV):
+                new.append(
+                    affine([row2(OUT + 5 * r + c, at) for c in range(NV)], held, total[pl.ds(CHORD * r + at, 1)])
+                )
+            held = new
+        return held
+
+    held = [jnp.zeros((1, LANES), F32) for _ in range(NV)]
+    for q in reversed(range(CHORD // 8)):
+        held = relay_back(q, held)
 
     for q in range(CHORD // 8):
         for kind in range(2):
             tile = zero
             for s in range(NV):
-                part_s = entry[pl.ds(CHORD * (NV * kind + s) + 8 * q, 8)]
+                part_s = (entry2 if kind else entry)[pl.ds(CHORD * s + 8 * q, 8)]
                 if s > 0:
                     part_s = pltpu.roll(part_s, 16 * s, 1)
                 tile = jnp.where(blk == s, part_s, tile)
@@ -363,14 +397,6 @@
 
     exchange(send2, recv2, 2, 1)
 
-    def gather_steps(step, _):
-        for index in range(NV * NV):
-            at = pl.ds(pl.multiple_of((step * NV * NV + index) * 8, 8), 8)
-            lows_by[at] = block(lowf, index, step)
-            upps_by[at] = block(uppf, index, step)
-        return 0
-
-    lax.fori_loop(0, HALF, gather_steps, 0)
     settle(recv2, (CHORD - 1) * 2, 3)
 
     for kind in range(2):
@@ -390,13 +416,13 @@
         carry[pl.ds(8 * (NV + v) + 1, NK, stride=2)] = c1[v]
 
     def by_step(ref, step, r):
-        return [ref[pl.ds(pl.multiple_of((step * NV * NV + NV * r + c) * 8, 8), 8)] for c in range(NV)]
+        return [block(ref, NV * r + c, step) for c in range(NV)]
 
     def sweep_ahead(step, held):
         new = []
         for r in range(NV):
             at = pl.ds(pl.multiple_of((step * NV + r) * 8, 8), 8)
-            val = residue(source[at], by_step(lows_by, step, r), held)
+            val = residue(source[at], by_step(lowf, step, r), held)
             ysweep[at] = val
             new.append(val)
         return tuple(new)
@@ -408,7 +434,7 @@
         new = []
         for r in range(NV):
             at = pl.ds(pl.multiple_of((step * NV + r) * 8, 8), 8)
-            val = residue(ysweep[at], by_step(upps_by, step, r), held)
+            val = residue(ysweep[at], by_step(uppf, step, r), held)
             wnat[pl.ds(128 * r + step, 8, stride=HALF)] = val
             new.append(val)
         return tuple(new)
@@ -504,8 +530,8 @@
         f32(88 * 8, LANES),
         f32(88 * NK, LANES),
         f32(CHORD * GROUPS, 1, LANES), f32(CHORD * GROUPS, 1, LANES),
-        f32(88 * CHORD, LANES),
-        f32(2 * NV * CHORD, LANES), f32(NV * CHORD, LANES),
+        f32(32 * CHORD, LANES), f32(55 * CHORD, LANES),
+        f32(NV * CHORD, LANES), f32(NV * CHORD, LANES), f32(NV * CHORD, LANES),
         f32(2 * CHORD, 1, LANES), f32(2 * CHORD, 1, LANES),
         f32(64, LANES), f32(80, LANES),
         f32(HALF * NV * 8, LANES), f32(narrow, LANES),
@@ -515,13 +541,13 @@
         f32(3 * NV, 1, LANES), f32(SPAN * 3 * NV, 1, LANES),
         f32(2 * NV, 1, LANES), f32(SPAN * 2 * NV, 1, LANES),
         f32(2 * SPAN * 8, LANES),
-        f32(wide, LANES), f32(wide, LANES), f32(narrow, LANES), f32(narrow, LANES), f32(narrow, LANES),
+        f32(narrow, LANES), f32(narrow, LANES), f32(narrow, LANES),
         pltpu.SemaphoreType.DMA((10,)),
         pltpu.SemaphoreType.DMA((8,)),
     ]
     out = pl.pallas_call(
         kernel,
-        out_shape=jax.ShapeDtypeStruct((narrow, LANES), F32),
+        out_shape=pltpu.VMEM((narrow, LANES), F32),
         in_specs=[pl.BlockSpec(memory_space=pl.ANY)] * 10,
         out_specs=pl.BlockSpec(memory_space=pltpu.VMEM),
         scratch_shapes=scratch,

time: 36.4 us -> 34 us (0.934)
  Pallas kernels: 34.6 us -> 33.2 us
  local copies, waits for them, and re-layouts: 1.72 us -> 0.73 us
    pallas_call x1, Pallas kernels: 34.6 us -> 33.2 us  [on_device(): pl.pallas_call(kernel, out_shape=pltpu.VMEM((narrow, LANES), F32), in_spe...]
    unnamed x1, local copies, waits for them, and re-layouts: 1.72 us -> 0.73 us
where the time goes in v3:
time: 34 us
  Pallas kernels  33.2 us (98%)
  local copies, waits for them, and re-layouts  0.73 us (2%)
    pallas_call x1, Pallas kernels, on_device(): pl.pallas_call(kernel, out_shape=pltpu.VMEM((narrow, LANES), F32), in_spe...  33.2 us
    unnamed x1, local copies, waits for them, and re-layouts  0.73 us

profile of v3, /device:TPU:1, one launch (start us, length us, event | category | flops | bytes accessed | tf_op | source)
XLA Modules:
  0.0 34.0 jit_solution(16983004913123865419)
XLA Ops:
  0.0 33.2 %shard_map.100 = f32[640,128]{1,0:T(8,128)S(1)} custom-call(f32[640,128]{1,0:T(8,128)} %bitcast.15, bf16[3200,128]{1,0:T(8,128)(2,1)} %bitcast.12, bf16[3200,128]{1,0:T(8,128)(2,1)} %bitcast.13, bf16[3200,128]{1,0:T(8,128)(2,1)} %bitcast.14, f32[640,128]{1,0:T(8,128)} %bitcast.16, f32[640,128]{1,0:T(8,128)} %bitcast.17, f32[640,128]{1,0:T(8,128)} %bitcast.18, ...), custom_call_target="tpu_custom_call" | custom-call | tf_op jit(solution)/shard_map/pallas_call | solution.py:548
  33.2 0.7 %copy.12 = f32[5,4,32,128]{3,2,1,0:T(8,128)} copy(f32[5,4,32,128]{3,2,1,0:T(8,128)S(1)} %bitcast.11) | data formatting | bytes 655360

commit v4 on v3

--- a/solution.py
+++ b/solution.py
@@ -74,6 +74,13 @@
             other = jnp.where(s_bit, down, up)
         tile = jnp.where(s_bit == b_bit, tile, other)
     return tile
+
+
+def skewed_transpose(tile, blk):
+    tile = pltpu.roll(tile, 0, 1, stride=16, stride_axis=0)
+    for d in (1, 2, 4):
+        tile = jnp.where((blk & d) != 0, pltpu.roll(tile, 8 - d, 0), tile)
+    return pltpu.roll(tile, 0, 1, stride=16, stride_axis=0)
 
 
 def kernel(
@@ -234,28 +241,28 @@
     for value in range(85, 88):
         put(value, jnp.zeros((NK, LANES), F32))
 
-    def shuffle(k, _):
+    def shuffle(k):
         for g in range(GROUPS):
             tile = comb[pl.ds(NK * 8 * g + k, 8, stride=NK)]
-            send1[pl.ds(8 * GROUPS * k + g, 8, stride=GROUPS), 0] = block_transpose(tile, sub, blk)
-        return 0
-
-    lax.fori_loop(0, NK, shuffle, 0)
+            send1[pl.ds(8 * GROUPS * k + g, 8, stride=GROUPS), 0] = skewed_transpose(tile, blk)
+
+    for k in range(NK):
+        shuffle(k)
 
     pl.semaphore_wait(barrier, CHORD - 1 + SPAN - 1)
 
-    def exchange(send, recv, rows, at):
+    def exchange(send, recv, rows, at, slot):
         for peer in CHORD_PEERS:
             to = chord_peer(peer)
             pltpu.make_async_remote_copy(
                 src_ref=send.at[pl.ds(to * rows, rows)],
-                dst_ref=recv.at[pl.ds(me_c * rows, rows)],
+                dst_ref=recv.at[pl.ds(slot * rows, rows)],
                 send_sem=sems.at[2 * at],
                 recv_sem=sems.at[2 * at + 1],
                 device_id={"chord": to},
                 device_id_type=MESH,
             ).start()
-        recv[pl.ds(me_c * rows, rows)] = send[pl.ds(me_c * rows, rows)]
+        recv[pl.ds(slot * rows, rows)] = send[pl.ds(me_c * rows, rows)]
 
     def spread(send, recv, rows, at):
         for o in SPAN_PEERS:
@@ -273,7 +280,7 @@
         whole = ref.at[pl.ds(0, rows)]
         pltpu.make_async_copy(whole, whole, sems.at[sem]).wait()
 
-    exchange(send1, recv1, GROUPS, 0)
+    exchange(send1, recv1, GROUPS, 0, me_c)
 
     for n, (src, dst) in enumerate([(spn, pt), (sln, lt), (sun, ut)]):
         loads[4 + n].wait()
@@ -395,7 +402,7 @@
                 tile = jnp.where(blk == s, part_s, tile)
             send2[pl.ds(16 * q + kind, 8, stride=2), 0] = tile
 
-    exchange(send2, recv2, 2, 1)
+    exchange(send2, recv2, 2, 1, me_c // 8 * 8 + lax.rem(8 - lax.rem(me_c, 8), 8))
 
     settle(recv2, (CHORD - 1) * 2, 3)
 
@@ -427,7 +434,7 @@
             new.append(val)
         return tuple(new)
 
-    lax.fori_loop(0, HALF, sweep_ahead, tuple(carry[tile_of(v)] for v in range(NV)), unroll=4)
+    lax.fori_loop(0, HALF, sweep_ahead, tuple(carry[tile_of(v)] for v in range(NV)), unroll=16)
 
     def sweep_back(n, held):
         step = HALF - 1 - n
@@ -439,7 +446,7 @@
             new.append(val)
         return tuple(new)
 
-    lax.fori_loop(0, HALF, sweep_back, tuple(carry[tile_of(NV + v)] for v in range(NV)), unroll=4)
+    lax.fori_loop(0, HALF, sweep_back, tuple(carry[tile_of(NV + v)] for v in range(NV)), unroll=16)
 
     for v in range(NV):
         turned = wnat[pl.ds(128 * v, 128)].T
@@ -491,7 +498,7 @@
         wt[at_j(j)] = wt[at_j(j)] + aa[at_j(j)] * a_in + cc[at_j(j)] * c_in
         return 0
 
-    lax.fori_loop(0, LANES, close, 0, unroll=8)
+    lax.fori_loop(0, LANES, close, 0, unroll=32)
 
     for n in range(7, 10):
         loads[n].wait()

time: 34 us -> 33.2 us (0.976)
  Pallas kernels: 33.2 us -> 32.4 us
    pallas_call x1, Pallas kernels: 33.2 us -> 32.4 us  [on_device(): pl.pallas_call(kernel, out_shape=pltpu.VMEM((narrow, LANES), F32), in_spe...]
where the time goes in v4:
time: 33.2 us; the launch traced here: 33.1 us
  Pallas kernels  32.4 us (98%)
  local copies, waits for them, and re-layouts  0.73 us (2%)
    pallas_call x1, Pallas kernels, on_device(): pl.pallas_call(kernel, out_shape=pltpu.VMEM((narrow, LANES), F32), in_spe...  32.4 us
    unnamed x1, local copies, waits for them, and re-layouts  0.73 us

profile of v4, /device:TPU:1, one launch (start us, length us, event | category | flops | bytes accessed | tf_op | source)
XLA Modules:
  0.0 33.1 jit_solution(15669647936516606900)
XLA Ops:
  0.0 32.4 %shard_map.100 = f32[640,128]{1,0:T(8,128)S(1)} custom-call(f32[640,128]{1,0:T(8,128)} %bitcast.15, bf16[3200,128]{1,0:T(8,128)(2,1)} %bitcast.12, bf16[3200,128]{1,0:T(8,128)(2,1)} %bitcast.13, bf16[3200,128]{1,0:T(8,128)(2,1)} %bitcast.14, f32[640,128]{1,0:T(8,128)} %bitcast.16, f32[640,128]{1,0:T(8,128)} %bitcast.17, f32[640,128]{1,0:T(8,128)} %bitcast.18, ...), custom_call_target="tpu_custom_call" | custom-call | tf_op jit(solution)/shard_map/pallas_call | solution.py:555
  32.4 0.7 %copy.12 = f32[5,4,32,128]{3,2,1,0:T(8,128)} copy(f32[5,4,32,128]{3,2,1,0:T(8,128)S(1)} %bitcast.11) | data formatting | bytes 655360

commit v5 on v4

--- a/solution.py
+++ b/solution.py
@@ -20,6 +20,7 @@
 GROUPS = 11
 MAT, VEC, OUT, INN, SRC = 0, 25, 30, 55, 80
 ZS, XS = 8, 4
+WIDE = NV * NV * 128
 
 
 def ring(step, size):
@@ -86,8 +87,8 @@
 def kernel(
     res_h, piv_h, low_h, upp_h, sp_h, sl_h, su_h, np_h, nl_h, nu_h,
     out_ref,
-    res, piv, low, upp, spn, sln, sun, npn, nln, nun,
-    pivf, lowf, uppf, source, state, comb, send1, recv1, expand, expand2, entry, entry2, total,
+    res, low, pair, spn, sln, sun, npn, nln, nun,
+    lowf, pairf, prefix, source, state, comb, send1, recv1, expand, expand2, entry, entry2, total,
     send2, recv2, unsh, carry, ysweep, wnat,
     wt, pt, lt, ut, gain, pre, alp, bet, cc, aa,
     gsend, grecv, hsend, hrecv, sentry,
@@ -110,7 +111,8 @@
 
     loads = {}
     for n, src, dst in [
-        (1, piv_h, piv), (0, res_h, res), (2, low_h, low), (3, upp_h, upp), (4, sp_h, spn), (5, sl_h, sln),
+        (2, low_h, low), (1, piv_h, pair.at[pl.ds(0, WIDE)]), (3, upp_h, pair.at[pl.ds(WIDE, WIDE)]),
+        (0, res_h, res), (4, sp_h, spn), (5, sl_h, sln),
         (6, su_h, sun), (7, np_h, npn), (8, nl_h, nln), (9, nu_h, nun),
     ]:
         copy = pltpu.make_async_copy(src, dst, load_sem.at[n])
@@ -125,21 +127,16 @@
     from_row = lax.broadcasted_iota(jnp.int32, (LANES, LANES), 1)
     order = jnp.where(from_row == HALF * lax.rem(to_row, 8) + to_row // 8, 1.0, 0.0).astype(jnp.bfloat16)
 
-    def widen(src, dst):
-        def body(n, _):
-            rows = pl.ds(pl.multiple_of(n * 128, 128), 128)
-            dst[rows] = jnp.dot(order, src[rows], preferred_element_type=F32)
-            return 0
-
-        lax.fori_loop(0, NV * NV, body, 0, unroll=5)
-
-    loads[1].wait()
-    widen(piv, pivf)
+    def widen(src, dst, n):
+        rows = pl.ds(pl.multiple_of(n * 128, 128), 128)
+        dst[rows] = jnp.dot(order, src[rows], preferred_element_type=F32)
+
+    def widen_low(n, _):
+        widen(low, lowf, n)
+        return 0
+
     loads[2].wait()
-    widen(low, lowf)
-    loads[3].wait()
-    widen(upp, uppf)
-    loads[0].wait()
+    lax.fori_loop(0, NV * NV, widen_low, 0, unroll=25)
 
     zero = jnp.zeros((8, LANES), F32)
 
@@ -155,55 +152,77 @@
     def blocks(ref, step):
         return [[block(ref, 5 * r + c, step) for c in range(NV)] for r in range(NV)]
 
-    def sources(step):
-        cells = [strided(res, c, step) for c in range(NV)]
-        src = [dot([block(pivf, 5 * r + c, step) for c in range(NV)], cells) for r in range(NV)]
-        for r in range(NV):
-            source[pl.ds(pl.multiple_of((step * NV + r) * 8, 8), 8)] = src[r]
-        return src
-
-    def map_step(step, odd):
-        src = sources(step)
+    def ahead_step(step):
         lows = blocks(lowf, step)
-        cols = []
         for c in range(NV):
             new = matvec(lows, [state[tile_of(MAT + 5 * r + c)] for r in range(NV)])
             for r in range(NV):
                 state[tile_of(MAT + 5 * r + c)] = new[r]
-            cols.append(new)
+                prefix[pl.ds(pl.multiple_of((5 * r + c) * 128 + 8 * step, 8), 8)] = new[r]
+
+    for index in range(NV * NV):
+        low_0 = block(lowf, index, 0)
+        state[tile_of(MAT + index)] = low_0
+        prefix[pl.ds(index * 128, 8)] = low_0
+    loads[1].wait()
+    loads[3].wait()
+
+    def ahead_steps(n, _):
+        for t in range(3):
+            ahead_step(3 * n + t + 1)
+        for t in range(10):
+            widen(pair, pairf, 10 * n + t)
+        return 0
+
+    lax.fori_loop(0, 5, ahead_steps, 0)
+    loads[0].wait()
+
+    def sources(step):
+        cells = [strided(res, c, step) for c in range(NV)]
+        src = [dot([block(pairf, 5 * r + c, step) for c in range(NV)], cells) for r in range(NV)]
+        for r in range(NV):
+            source[pl.ds(pl.multiple_of((step * NV + r) * 8, 8), 8)] = src[r]
+        return src
+
+    def upper(index, step):
+        return block(pairf, NV * NV + index, step)
+
+    def back_step(step, odd):
+        src = sources(step)
+        lows = blocks(lowf, step)
         vec = [state[tile_of(VEC + r)] for r in range(NV)]
         new = [affine(lows[r], vec, src[r]) if odd else -residue(src[r], lows[r], vec) for r in range(NV)]
         for r in range(NV):
             state[tile_of(VEC + r)] = new[r]
-        cols.append(new)
-        upps = blocks(uppf, step)
+        mats = blocks(prefix, step)
         for r in range(NV):
             row = [state[tile_of(OUT + 5 * r + c)] for c in range(NV)]
             for c in range(NV):
                 at = tile_of(INN + 5 * r + c)
-                state[at] = affine(row, cols[c], state[at])
+                state[at] = affine(row, column(mats, c), state[at])
             at = tile_of(SRC + r)
-            state[at] = affine(row, cols[NV], state[at])
+            state[at] = affine(row, new, state[at])
+        upps = [[upper(5 * r + c, step) for c in range(NV)] for r in range(NV)]
+        for r in range(NV):
+            row = [state[tile_of(OUT + 5 * r + c)] for c in range(NV)]
             for c in range(NV):
                 state[tile_of(OUT + 5 * r + c)] = dot(row, column(upps, c))
 
     first = sources(0)
     for r in range(NV):
         for c in range(NV):
-            low = block(lowf, 5 * r + c, 0)
-            state[tile_of(MAT + 5 * r + c)] = low
-            state[tile_of(INN + 5 * r + c)] = low
-            state[tile_of(OUT + 5 * r + c)] = block(uppf, 5 * r + c, 0)
+            state[tile_of(INN + 5 * r + c)] = block(lowf, 5 * r + c, 0)
+            state[tile_of(OUT + 5 * r + c)] = upper(5 * r + c, 0)
         state[tile_of(VEC + r)] = -first[r]
         state[tile_of(SRC + r)] = -first[r]
-    map_step(1, True)
-
-    def map_pair(pair, _):
-        map_step(2 * pair, False)
-        map_step(2 * pair + 1, True)
+    back_step(1, True)
+
+    def back_pair(n, _):
+        back_step(2 * n, False)
+        back_step(2 * n + 1, True)
         return 0
 
-    lax.fori_loop(1, HALF // 2, map_pair, 0)
+    lax.fori_loop(1, HALF // 2, back_pair, 0)
 
     def half(value, which):
         return state[pl.ds(8 * value + which, NK, stride=2)]
@@ -441,7 +460,7 @@
         new = []
         for r in range(NV):
             at = pl.ds(pl.multiple_of((step * NV + r) * 8, 8), 8)
-            val = residue(ysweep[at], by_step(uppf, step, r), held)
+            val = residue(ysweep[at], by_step(pairf, step, r + NV), held)
             wnat[pl.ds(128 * r + step, 8, stride=HALF)] = val
             new.append(val)
         return tuple(new)
@@ -529,10 +548,10 @@
     b16 = lambda *shape: pltpu.VMEM(shape, jnp.bfloat16)
     wide, narrow = NV * NV * 128, NV * 128
     scratch = [
-        f32(narrow, LANES), b16(wide, LANES), b16(wide, LANES), b16(wide, LANES),
+        f32(narrow, LANES), b16(wide, LANES), b16(2 * wide, LANES),
         f32(narrow, LANES), f32(narrow, LANES), f32(narrow, LANES),
         b16(narrow, LANES), b16(narrow, LANES), b16(narrow, LANES),
-        f32(wide, LANES), f32(wide, LANES), f32(wide, LANES),
+        f32(wide, LANES), f32(2 * wide, LANES), f32(wide, LANES),
         f32(HALF * NV * 8, LANES),
         f32(88 * 8, LANES),
         f32(88 * NK, LANES),

time: 33.2 us -> 31.7 us (0.955)
  Pallas kernels: 32.4 us -> 30.9 us
    pallas_call x1, Pallas kernels: 32.4 us -> 30.9 us  [on_device(): pl.pallas_call(kernel, out_shape=pltpu.VMEM((narrow, LANES), F32), in_spe...]
where the time goes in v5:
time: 31.7 us
  Pallas kernels  30.9 us (97%)
  local copies, waits for them, and re-layouts  0.73 us (2%)
    pallas_call x1, Pallas kernels, on_device(): pl.pallas_call(kernel, out_shape=pltpu.VMEM((narrow, LANES), F32), in_spe...  30.9 us
    unnamed x1, local copies, waits for them, and re-layouts  0.73 us

profile of v5, /device:TPU:1, one launch (start us, length us, event | category | flops | bytes accessed | tf_op | source)
XLA Modules:
  0.0 31.7 jit_solution(5236480278914781307)
XLA Ops:
  0.0 30.9 %shard_map.100 = f32[640,128]{1,0:T(8,128)S(1)} custom-call(f32[640,128]{1,0:T(8,128)} %bitcast.15, bf16[3200,128]{1,0:T(8,128)(2,1)} %bitcast.12, bf16[3200,128]{1,0:T(8,128)(2,1)} %bitcast.13, bf16[3200,128]{1,0:T(8,128)(2,1)} %bitcast.14, f32[640,128]{1,0:T(8,128)} %bitcast.16, f32[640,128]{1,0:T(8,128)} %bitcast.17, f32[640,128]{1,0:T(8,128)} %bitcast.18, ...), custom_call_target="tpu_custom_call" | custom-call | tf_op jit(solution)/shard_map/pallas_call | solution.py:574
  30.9 0.7 %copy.12 = f32[5,4,32,128]{3,2,1,0:T(8,128)} copy(f32[5,4,32,128]{3,2,1,0:T(8,128)S(1)} %bitcast.11) | data formatting | bytes 655360

commit v6 on v5

--- a/solution.py
+++ b/solution.py
@@ -61,20 +61,6 @@
 
 def matvec(lhs, vec):
     return [dot(row, vec) for row in lhs]
-
-
-def block_transpose(tile, sub, blk):
-    for d in (4, 2, 1):
-        s_bit = (sub & d) != 0
-        b_bit = (blk & d) != 0
-        if d == 4:
-            other = pltpu.roll(pltpu.roll(tile, 4, 0), 64, 1)
-        else:
-            up = pltpu.roll(pltpu.roll(tile, 8 - d, 0), 16 * d, 1)
-            down = pltpu.roll(pltpu.roll(tile, d, 0), 128 - 16 * d, 1)
-            other = jnp.where(s_bit, down, up)
-        tile = jnp.where(s_bit == b_bit, tile, other)
-    return tile
 
 
 def skewed_transpose(tile, blk):
@@ -119,7 +105,6 @@
         copy.start()
         loads[n] = copy
 
-    sub = lax.broadcasted_iota(jnp.int32, (8, LANES), 0)
     lane = lax.broadcasted_iota(jnp.int32, (8, LANES), 1)
     blk = lane // 16
 
@@ -131,12 +116,12 @@
         rows = pl.ds(pl.multiple_of(n * 128, 128), 128)
         dst[rows] = jnp.dot(order, src[rows], preferred_element_type=F32)
 
-    def widen_low(n, _):
-        widen(low, lowf, n)
-        return 0
-
     loads[2].wait()
-    lax.fori_loop(0, NV * NV, widen_low, 0, unroll=25)
+    for n in range(NV):
+        rows = [pl.ds(128 * (NV * n + c), 128) for c in range(NV)]
+        abreast = jnp.dot(order, jnp.concatenate([low[at] for at in rows], axis=1), preferred_element_type=F32)
+        for c in range(NV):
+            lowf[rows[c]] = abreast[:, 128 * c : 128 * c + 128]
 
     zero = jnp.zeros((8, LANES), F32)
 
@@ -428,9 +413,9 @@
     for kind in range(2):
         for k in range(NK):
             tile = recv2[pl.ds(16 * k + kind, 8, stride=2), 0]
-            unsh[pl.ds(8 * (NK * kind + k), 8)] = block_transpose(tile, sub, blk)
-    a0 = [unsh[pl.ds(v, NK, stride=8)] for v in range(NV)]
-    c1 = [unsh[pl.ds(8 * NK + v, NK, stride=8)] for v in range(NV)]
+            unsh[pl.ds(8 * (NK * kind + k), 8)] = skewed_transpose(tile, blk)
+    a0 = [unsh[pl.ds((8 - v) % 8, NK, stride=8)] for v in range(NV)]
+    c1 = [unsh[pl.ds(8 * NK + (8 - v) % 8, NK, stride=8)] for v in range(NV)]
     a1 = [m + half(VEC + r, 0) for r, m in enumerate(matvec(half_matrix(MAT, 0), a0))]
     back = matvec(half_matrix(OUT, 1), c1)
     fore = matvec(half_matrix(INN, 1), a1)

time: 31.7 us -> 31.7 us (level)
  no operation moved by 1% of the time
where the time goes in v6:
time: 31.7 us; the launch traced here: 31.6 us
  Pallas kernels  30.9 us (97%)
  local copies, waits for them, and re-layouts  0.73 us (2%)
    pallas_call x1, Pallas kernels, on_device(): pl.pallas_call(kernel, out_shape=pltpu.VMEM((narrow, LANES), F32), in_spe...  30.9 us
    unnamed x1, local copies, waits for them, and re-layouts  0.73 us

profile of v6, /device:TPU:1, one launch (start us, length us, event | category | flops | bytes accessed | tf_op | source)
XLA Modules:
  0.0 31.6 jit_solution(1546312775883161708)
XLA Ops:
  0.0 30.9 %shard_map.100 = f32[640,128]{1,0:T(8,128)S(1)} custom-call(f32[640,128]{1,0:T(8,128)} %bitcast.15, bf16[3200,128]{1,0:T(8,128)(2,1)} %bitcast.12, bf16[3200,128]{1,0:T(8,128)(2,1)} %bitcast.13, bf16[3200,128]{1,0:T(8,128)(2,1)} %bitcast.14, f32[640,128]{1,0:T(8,128)} %bitcast.16, f32[640,128]{1,0:T(8,128)} %bitcast.17, f32[640,128]{1,0:T(8,128)} %bitcast.18, ...), custom_call_target="tpu_custom_call" | custom-call | tf_op jit(solution)/shard_map/pallas_call | solution.py:559
  30.9 0.7 %copy.12 = f32[5,4,32,128]{3,2,1,0:T(8,128)} copy(f32[5,4,32,128]{3,2,1,0:T(8,128)S(1)} %bitcast.11) | data formatting | bytes 655360

commit v7 on v6

--- a/solution.py
+++ b/solution.py
@@ -89,21 +89,23 @@
     def chord_peer(peer):
         return lax.rem(z + peer[0], ZS) * XS + lax.rem(x + peer[1], XS)
 
-    barrier = pltpu.get_barrier_semaphore()
-    for peer in CHORD_PEERS:
-        pl.semaphore_signal(barrier, inc=1, device_id={"chord": chord_peer(peer)}, device_id_type=MESH)
-    for o in SPAN_PEERS:
-        pl.semaphore_signal(barrier, inc=1, device_id={"span": lax.rem(me_s + o, SPAN)}, device_id_type=MESH)
-
     loads = {}
     for n, src, dst in [
         (2, low_h, low), (1, piv_h, pair.at[pl.ds(0, WIDE)]), (3, upp_h, pair.at[pl.ds(WIDE, WIDE)]),
         (0, res_h, res), (4, sp_h, spn), (5, sl_h, sln),
         (6, su_h, sun), (7, np_h, npn), (8, nl_h, nln), (9, nu_h, nun),
     ]:
-        copy = pltpu.make_async_copy(src, dst, load_sem.at[n])
-        copy.start()
-        loads[n] = copy
+        loads[n] = pltpu.make_async_copy(src, dst, load_sem.at[n])
+    for n in (2, 1, 3, 0):
+        loads[n].start()
+
+    barrier = pltpu.get_barrier_semaphore()
+    for peer in CHORD_PEERS:
+        pl.semaphore_signal(barrier, inc=1, device_id={"chord": chord_peer(peer)}, device_id_type=MESH)
+    for o in SPAN_PEERS:
+        pl.semaphore_signal(barrier, inc=1, device_id={"span": lax.rem(me_s + o, SPAN)}, device_id_type=MESH)
+    for n in range(4, 10):
+        loads[n].start()
 
     lane = lax.broadcasted_iota(jnp.int32, (8, LANES), 1)
     blk = lane // 16

time: 31.7 us -> 31.5 us (level)
  no operation moved by 1% of the time
where the time goes in v7:
time: 31.5 us; the launch traced here: 31.4 us
  Pallas kernels  30.7 us (97%)
  local copies, waits for them, and re-layouts  0.73 us (2%)
    pallas_call x1, Pallas kernels, on_device(): pl.pallas_call(kernel, out_shape=pltpu.VMEM((narrow, LANES), F32), in_spe...  30.7 us
    unnamed x1, local copies, waits for them, and re-layouts  0.73 us

profile of v7, /device:TPU:1, one launch (start us, length us, event | category | flops | bytes accessed | tf_op | source)
XLA Modules:
  0.0 31.4 jit_solution(4352103152533293583)
XLA Ops:
  0.0 30.7 %shard_map.100 = f32[640,128]{1,0:T(8,128)S(1)} custom-call(f32[640,128]{1,0:T(8,128)} %bitcast.15, bf16[3200,128]{1,0:T(8,128)(2,1)} %bitcast.12, bf16[3200,128]{1,0:T(8,128)(2,1)} %bitcast.13, bf16[3200,128]{1,0:T(8,128)(2,1)} %bitcast.14, f32[640,128]{1,0:T(8,128)} %bitcast.16, f32[640,128]{1,0:T(8,128)} %bitcast.17, f32[640,128]{1,0:T(8,128)} %bitcast.18, ...), custom_call_target="tpu_custom_call" | custom-call | tf_op jit(solution)/shard_map/pallas_call | solution.py:561
  30.7 0.7 %copy.12 = f32[5,4,32,128]{3,2,1,0:T(8,128)} copy(f32[5,4,32,128]{3,2,1,0:T(8,128)S(1)} %bitcast.11) | data formatting | bytes 655360
